TPU v7x, 512 devices: a whole 4x8x8 slice. The times are simulated.
512 devices in a mesh: band: 128 (over y, z, core), chan: 4 (over x).
Axes of the slice: x: 4, y: 8, z: 8, core: 2. Of those that a mesh axis runs over, the one named last changes fastest.
Arguments:
- atmos: bfloat16 [12, 512, 1440], P('chan', 'band'), may hold values from -6 to 6
- remap_lat: bfloat16 [32768, 64, 4], P('band'), may hold values from -3 to 3
- remap_lon: bfloat16 [32768, 32, 64], P('band'), may hold values from -0.09375 to 0.09375
- pair_tile: int32 [32768, 1], P('band'), may hold values from 0 to 255; in each aligned block of 256 rows (0 to 255, 256 to 511, ...) at most 2 rows name the same one
- pair_col: int32 [32768], P('band'), may hold values from 0 to 1408
- tile_owner: int32 [256], replicated, may hold values from 0 to 255, each once
- neighbours: int32 [256, 4], replicated, may hold values from -1 to 255, as said below
- land_mask: int32 [256, 4096], P('band'), may hold values 0 or 1
- stem_w: bfloat16 [12, 192], P(None, 'chan'), may hold values from -1.75 to 1.75
- dw_w: bfloat16 [192, 49], P('chan'), may hold values from -0.875 to 0.875
- ln_gain: bfloat16 [192], P('chan'), may hold values from 0.099609375 to 1.8984375
- w_in: bfloat16 [768, 192], P('chan'), may hold values from -0.4375 to 0.4375
- b_in: bfloat16 [768], P('chan'), may hold values from -3 to 3
- w_out: bfloat16 [768, 192], P('chan'), may hold values from -0.21875 to 0.21875
- head_w: bfloat16 [192], P('chan'), may hold values from -0.4375 to 0.4375
Outputs:
- sst: float32 [256, 4096], P('band')
Inputs may be any that keep to these rules, and one draw needn't show every extreme that they name: `pair_tile`: the pairs of one band device (aligned blocks of 256 rows) name any one tile at most 2 times; every tile is named by some pair. `tile_owner`: each place once. `neighbours`: tiles form a grid of 4 rows of 64 tiles that closes west to east; -1 only north of the first row and south of the last; if u is the north neighbour of t then t is the south neighbour of u, and likewise west and east.
All inputs are finite; a program needn't handle non-finite values. No bound on the sum of `land_mask` on one device may be relied on, other than what follows from the above.
Results may differ from a plain program's by a relative error of at most 0.023.
Values may be sent and summed in bfloat16 or wider, within the bound.
A program may use at most 64 MiB of HBM per device.

v0:
```python
import jax
import jax.numpy as jnp
from jax import lax
from jax.sharding import PartitionSpec as P


def depthwise(features, kernel, rows, side):
    wide = side + 6
    flat_rows = jnp.pad(features.astype(jnp.float32), ((0, 0), (0, 0), (0, 8)))
    total = jnp.zeros((features.shape[0], features.shape[1], rows * wide), jnp.float32)
    for row_shift in range(7):
        for col_shift in range(7):
            offset = row_shift * wide + col_shift
            weight_col = kernel[:, row_shift * 7 + col_shift].astype(jnp.float32)
            total = (
                total + weight_col[:, None, None] * flat_rows[:, :, offset : offset + rows * wide]
            )
    total = total.reshape(features.shape[0], features.shape[1], rows, wide)[..., :side]
    return total.reshape(features.shape[0], features.shape[1], rows * side)


def assemble(fluxes, above, below, lefts, rights):
    middle = jnp.concatenate([lefts, fluxes, rights], axis=-1)
    top_rows = jnp.pad(above, ((0, 0), (0, 0), (0, 0), (3, 3)))
    bottom_rows = jnp.pad(below, ((0, 0), (0, 0), (0, 0), (3, 3)))
    return jnp.concatenate([top_rows, middle, bottom_rows], axis=2)


def normalize(values, sums, squares, gain, width):
    mean_val = sums / width
    variance = squares / width - mean_val * mean_val
    scaled = (values - mean_val[None, :]) * lax.rsqrt(variance + 1e-06)[None, :]
    return (scaled * gain.astype(jnp.float32)[:, None]).astype(jnp.bfloat16)


def channel_features(fields, stem_w, dw_w, tiles_here, side):
    wide = side + 6
    features = jnp.einsum("qfp,fc->cqp", fields, stem_w, preferred_element_type=jnp.float32).astype(
        jnp.bfloat16
    )
    local_width = features.shape[0]
    mixed = depthwise(features, dw_w, side, side).astype(jnp.bfloat16).reshape(local_width, -1)
    inner = features.reshape(local_width, tiles_here, wide, wide)[:, :, 3 : 3 + side, 3 : 3 + side]
    return (mixed, inner.reshape(local_width, -1))


def body(
    atmos,
    remap_lat,
    remap_lon,
    pair_tile,
    pair_col,
    tile_owner,
    neighbours,
    land_mask,
    stem_w,
    dw_w,
    ln_gain,
    w_in,
    b_in,
    w_out,
    head_w,
):
    band_count = lax.axis_size("band")
    chan_count = lax.axis_size("chan")
    band_here = lax.axis_index("band")
    local_fields, band_rows, longitudes = atmos.shape
    pair_count = pair_col.shape[0]
    side = remap_lat.shape[1]
    window = remap_lon.shape[1]
    tile_total = tile_owner.shape[0]
    tiles_here = tile_total // band_count
    capacity = max(2, pair_count // band_count)
    tile_iota = jnp.arange(tile_total, dtype=jnp.int32)
    pair_tiles = pair_tile[:, 0]
    places = jnp.sum(
        jnp.where(pair_tiles[:, None] == tile_iota[None, :], tile_owner[None, :], 0), axis=1
    )
    pair_iota = jnp.arange(pair_count, dtype=jnp.int32)
    earlier = (pair_tiles[:, None] == pair_tiles[None, :]) & (
        pair_iota[:, None] > pair_iota[None, :]
    )
    ranks = jnp.sum(earlier.astype(jnp.int32), axis=1)
    slots = places * capacity + ranks
    zero_index = jnp.int32(0)
    windows = jax.vmap(
        lambda start_col: lax.dynamic_slice(
            atmos, (zero_index, zero_index, start_col), (local_fields, band_rows, window)
        )
    )(pair_col)
    total_slots = band_count * tiles_here * capacity

    def place_rows(values):
        flat_rows = values.reshape(pair_count, -1)
        filled = (
            jnp.zeros((total_slots, flat_rows.shape[1]), flat_rows.dtype).at[slots].set(flat_rows)
        )
        return filled.reshape(band_count, tiles_here * capacity, flat_rows.shape[1])

    got_windows, got_lat, got_lon = (
        lax.all_to_all(place_rows(windows), "band", split_axis=0, concat_axis=0, tiled=True),
        lax.all_to_all(place_rows(remap_lat), "band", split_axis=0, concat_axis=0, tiled=True),
        lax.all_to_all(place_rows(remap_lon), "band", split_axis=0, concat_axis=0, tiled=True),
    )
    lead = (band_count, tiles_here, capacity)
    window_blocks = got_windows.reshape(lead + (local_fields, band_rows, window))
    lat_blocks = got_lat.reshape(lead + (side, band_rows))
    lon_blocks = got_lon.reshape(lead + (window, side))
    partial_rows = jnp.einsum(
        "sqkfrc,sqkcj->sqkfrj", window_blocks, lon_blocks, preferred_element_type=jnp.float32
    )
    remapped = jnp.einsum(
        "sqkir,sqkfrj->qfij",
        lat_blocks.astype(jnp.float32),
        partial_rows,
        precision=lax.Precision.HIGHEST,
    )
    mask_here = land_mask.astype(jnp.float32)
    fluxes = (remapped * mask_here.reshape(tiles_here, 1, side, side)).astype(jnp.bfloat16)
    strips = jnp.concatenate(
        [
            fluxes[:, :, :3, :].reshape(tiles_here, local_fields, 3 * side),
            fluxes[:, :, side - 3 :, :].reshape(tiles_here, local_fields, 3 * side),
            fluxes[:, :, :, :3].reshape(tiles_here, local_fields, 3 * side),
            fluxes[:, :, :, side - 3 :].reshape(tiles_here, local_fields, 3 * side),
        ],
        axis=2,
    )
    my_places = band_here * tiles_here + jnp.arange(tiles_here, dtype=jnp.int32)
    my_tiles = jnp.sum(
        jnp.where(tile_owner[None, :] == my_places[:, None], tile_iota[None, :], 0), axis=1
    )
    near_ids = jnp.sum(
        jnp.where((tile_iota[None, :] == my_tiles[:, None])[:, :, None], neighbours[None, :, :], 0),
        axis=1,
    )
    near_places = jnp.where(
        near_ids >= 0,
        jnp.sum(
            jnp.where(
                near_ids[:, :, None] == tile_iota[None, None, :], tile_owner[None, None, :], 0
            ),
            axis=2,
        ),
        -1,
    )
    piece = lax.all_gather(strips, "band", axis=0, tiled=True)
    rows_iota = jnp.arange(piece.shape[0], dtype=jnp.int32)
    select = (near_places[:, :, None] == rows_iota[None, None, :]).astype(jnp.bfloat16)
    fetched = jnp.einsum("qkn,nfl->qkfl", select, piece, preferred_element_type=jnp.float32)
    fetched = fetched.astype(jnp.bfloat16).reshape(tiles_here, 4, local_fields, 4, 3 * side)
    above = fetched[:, 0, :, 1].reshape(tiles_here, local_fields, 3, side)
    below = fetched[:, 1, :, 0].reshape(tiles_here, local_fields, 3, side)
    lefts = fetched[:, 2, :, 3].reshape(tiles_here, local_fields, side, 3)
    rights = fetched[:, 3, :, 2].reshape(tiles_here, local_fields, side, 3)
    framed = assemble(fluxes, above, below, lefts, rights)
    wide = side + 6
    fields = lax.all_gather(
        framed.reshape(tiles_here, local_fields, wide * wide), "chan", axis=1, tiled=True
    )
    mask_flat = mask_here.reshape(-1)
    mixed, inner = channel_features(fields, stem_w, dw_w, tiles_here, side)
    local_width = mixed.shape[0]
    width = local_width * chan_count
    values = mixed.astype(jnp.float32)
    sums, squares = (
        lax.psum(jnp.sum(values, axis=0).astype(jnp.bfloat16), "chan").astype(jnp.float32),
        lax.psum(jnp.sum(values * values, axis=0).astype(jnp.bfloat16), "chan").astype(jnp.float32),
    )
    normed = normalize(values, sums, squares, ln_gain, width)
    columns = w_in
    before = jnp.dot(
        columns,
        lax.all_gather(normed, "chan", axis=0, tiled=True),
        preferred_element_type=jnp.float32,
    )
    activated = jax.nn.gelu(before + b_in.astype(jnp.float32)[:, None]).astype(jnp.bfloat16)
    columns = w_out
    down = lax.psum_scatter(
        jnp.einsum("hc,hp->cp", columns, activated, preferred_element_type=jnp.float32).astype(
            jnp.bfloat16
        ),
        "chan",
        scatter_dimension=0,
        tiled=True,
    ).astype(jnp.float32)
    state = inner.astype(jnp.float32) + down
    head_part = jnp.sum(head_w.astype(jnp.float32)[:, None] * state, axis=0)
    result = lax.psum(head_part.astype(jnp.bfloat16), "chan").astype(jnp.float32) * mask_flat
    return result.reshape(tiles_here, side * side)


def solution(mesh):
    return jax.shard_map(
        body,
        mesh=mesh,
        in_specs=(
            P("chan", "band", None),
            P("band", None, None),
            P("band", None, None),
            P("band", None),
            P("band"),
            P(),
            P(),
            P("band", None),
            P(None, "chan"),
            P("chan", None),
            P("chan"),
            P("chan", None),
            P("chan"),
            P("chan", None),
            P("chan"),
        ),
        out_specs=P("band", None),
        check_vma=False,
    )
```

profile of v0, /device:TPU:8, one launch (start us, length us, event | category | flops | bytes accessed | tf_op | source)
XLA Modules:
  0.0 427.6 jit_solution(17746219138270675631)
XLA Ops:
  8.6 1.5 scatter_custom_fusion.2
  10.9 17.4 %all-to-all-start.2 = ((bf16[128,4,256]{2,1,0:T(4,128)(2,1)}), bf16[128,4,256]{2,1,0:T(4,128)(2,1)S(1)}, u32[]{:S(2)}, u32[]{:S(2)}) async-start(bf16[128,4,256]{2,1,0:T(4,128)(2,1)} %reshape.488), calls=%async_computation.2 | async-start | bytes 524288 | tf_op jit(solution)/shard_map/all_to_all | solution.py:102
  28.3 1.7 copy.111
  30.1 14.7 %gather_fusion = bf16[256,3,4,32]{2,1,3,0:T(4,128)(2,1)} fusion(bf16[3,4,1440]{1,0,2:T(4,128)(2,1)S(1)} %copy.111, s32[256]{0:T(256)S(1)} %fusion.96), kind=kCustom, calls=%fused_computation | custom fusion | bytes 396288 | tf_op jit(solution)/shard_map/vmap()/gather | solution.py:87
  44.8 10.0 %copy.112 = bf16[256,3,4,32]{0,3,2,1:T(8,128)(2,1)S(1)} copy(bf16[256,3,4,32]{2,1,3,0:T(4,128)(2,1)} %gather_fusion) | data formatting | bytes 393216 | tf_op jit(solution)/shard_map/vmap()/gather | solution.py:87
  54.9 1.6 scatter_custom_fusion
  57.4 14.3 %all-to-all-start = ((bf16[128,4,384]{2,1,0:T(4,128)(2,1)}), bf16[128,4,384]{2,1,0:T(4,128)(2,1)S(1)}, u32[]{:S(2)}, u32[]{:S(2)}) async-start(bf16[128,4,384]{2,1,0:T(4,128)(2,1)} %reshape.482), calls=%async_computation | async-start | bytes 786432 | tf_op jit(solution)/shard_map/all_to_all | solution.py:101
  73.2 3.5 scatter_custom_fusion.1
  76.7 2.2 reshape.485
  78.9 10.2 %all-to-all-done = bf16[128,4,384]{2,1,0:T(4,128)(2,1)S(1)} async-done(((bf16[128,4,384]{2,1,0:T(4,128)(2,1)}), bf16[128,4,384]{2,1,0:T(4,128)(2,1)S(1)}, u32[]{:S(2)}, u32[]{:S(2)}) %all-to-all-start) | async-done | bytes 393248 | tf_op jit(solution)/shard_map/all_to_all | solution.py:101
  89.1 7.6 %all-to-all-start.1 = ((bf16[128,4,2048]{2,1,0:T(4,128)(2,1)}), bf16[128,4,2048]{2,1,0:T(4,128)(2,1)}, u32[]{:S(2)}, u32[]{:S(2)}) async-start(bf16[128,4,2048]{2,1,0:T(4,128)(2,1)} %reshape.485), calls=%async_computation.1 | async-start | bytes 4194304 | tf_op jit(solution)/shard_map/all_to_all | solution.py:103
  97.5 2.5 copy.117
  100.0 48.8 %all-to-all-done.1 = bf16[128,4,2048]{2,1,0:T(4,128)(2,1)} async-done(((bf16[128,4,2048]{2,1,0:T(4,128)(2,1)}), bf16[128,4,2048]{2,1,0:T(4,128)(2,1)}, u32[]{:S(2)}, u32[]{:S(2)}) %all-to-all-start.1) | async-done | bytes 2097184 | tf_op jit(solution)/shard_map/all_to_all | solution.py:103
  148.8 3.4 copy.116
  152.2 6.5 %copy.141 = bf16[128,2,2,32,64,1]{4,3,5,2,1,0:T(8,128)(2,1)} copy(bf16[128,2,2,32,64,1]{0,4,3,2,1,5:T(8,128)(2,1)S(1)} %bitcast.73) | data formatting | bytes 4194304 | tf_op jit(solution)/shard_map/reshape | solution.py:108
  158.7 3.9 fusion.107
  162.6 2.0 fusion.71
  167.9 75.1 %all-gather.3.cloned.1.call-done = bf16[256,3,768]{2,1,0:T(4,128)(2,1)} async-done(((bf16[2,3,768]{2,1,0:T(4,128)(2,1)}), bf16[256,3,768]{2,1,0:T(4,128)(2,1)}) %all-gather.3.cloned.1.call-update) | async-done | bytes 1179664 | tf_op jit(solution)/shard_map/all_gather | solution.py:147
  243.0 1.7 fusion.74
  245.9 12.5 %all_gather.10 = bf16[2,12,4900]{2,0,1:T(2,128)(2,1)S(1)} all-gather(bf16[2,3,4900]{2,0,1:T(2,128)(2,1)S(1)} %copy.153), channel_id=1, replica_groups=mesh['band'=128,'chan'=4] {'chan'}, dimensions={1}, use_global_device_ids=true | all-gather | bytes 294000 | tf_op jit(solution)/shard_map/all_gather | solution.py:158
  258.9 22.8 %fusion.19 = bf16[48,2,4480]{2,0,1:T(8,128)(2,1)} fusion(f32[48,2,4900]{2,0,1:T(8,128)S(1)} %get-tuple-element.72, f32[48]{0:T(128)S(1)} %get-tuple-element.56, f32[48]{0:T(128)S(1)} %get-tuple-element.57, f32[48]{0:T(128)S(1)} %get-tuple-element.10, f32[48]{0:T(128)S(1)} %get-tuple-element.11, f32[48]{0:T(128)S(1)} %get-tuple-element.12, ...), kind=kLoop, calls=%fused_computation.30 | loop fusion | flops 42147840 | bytes 76775936 | tf_op jit(solution)/shard_map/add | solution.py:16
  281.8 6.1 %reshape.497 = bf16[48,2,64,70]{3,2,0,1:T(8,128)(2,1)S(1)} reshape(bf16[48,2,4480]{2,0,1:T(8,128)(2,1)} %fusion.19) | data formatting | bytes 1720320 | tf_op jit(solution)/shard_map/reshape | solution.py:18
  287.8 2.1 fusion.101
  290.6 2.4 reshape.550
  293.0 17.2 %all-reduce.4 = (bf16[8192]{0:T(1024)(128)(2,1)S(1)}, bf16[8192]{0:T(1024)(128)(2,1)S(1)}) all-reduce(bf16[8192]{0:T(1024)(128)(2,1)S(1)} %convert_element_type.697, bf16[8192]{0:T(1024)(128)(2,1)S(1)} %reduce_sum.83), channel_id=1, replica_groups=mesh['band'=128,'chan'=4] {'chan'}, use_global_device_ids=true, to_apply=%region_11.12 | all-reduce | flops 16384 | bytes 65536 | tf_op jit(solution)/shard_map/psum | solution.py:168
  311.7 40.7 %all-gather.5.cloned.1.call-done = bf16[192,8192]{1,0:T(8,128)(2,1)} async-done(((bf16[48,8192]{1,0:T(8,128)(2,1)}), bf16[192,8192]{1,0:T(8,128)(2,1)}) %all-gather.5.cloned.1.call-update) | async-done | bytes 3145744 | tf_op jit(solution)/shard_map/all_gather | solution.py:174
  352.3 6.9 %fusion.1 = bf16[192,8192]{1,0:T(8,128)(2,1)} fusion(bf16[192,192]{1,0:T(8,128)(2,1)S(1)} %copy-done, bf16[192,192]{1,0:T(8,128)(2,1)S(1)} %copy-done.9, bf16[192,8192]{1,0:T(8,128)(2,1)} %all-gather.5.cloned.1.call-done, f32[192]{0:T(256)S(1)} %convert_element_type.701), kind=kOutput, calls=%fused_computation.7 | convolution fusion | flops 1225261056 | bytes 6439680 | tf_op jit(solution)/shard_map/hc,hp->cp/dot_general | solution.py:180
  359.9 1.8 reshape.496
  362.9 1.9 reshape.500
  364.8 38.4 %reduce-scatter.2.cloned.1.call-done = bf16[48,8192]{1,0:T(8,128)(2,1)} async-done(((bf16[192,8192]{1,0:T(8,128)(2,1)}), bf16[48,8192]{1,0:T(8,128)(2,1)}) %reduce-scatter.2.cloned.1.call-update) | async-done | bytes 786448 | tf_op jit(solution)/shard_map/reduce_scatter | solution.py:179
  403.3 1.9 multiply_reduce_fusion.1
  405.2 15.0 %psum.23 = bf16[8192]{0:T(1024)(128)(2,1)S(1)} all-reduce(bf16[8192]{0:T(1024)(128)(2,1)S(1)} %multiply_reduce_fusion.1), channel_id=1, replica_groups=mesh['band'=128,'chan'=4] {'chan'}, use_global_device_ids=true, to_apply=%region_14.15 | all-reduce | flops 8192 | bytes 32768 | tf_op jit(solution)/shard_map/psum | solution.py:189
  (91 shorter events, 15.3 us)
Async XLA Ops:
  6.5 345.8 %copy-start = (bf16[192,192]{1,0:T(8,128)(2,1)S(1)}, bf16[192,192]{1,0:T(8,128)(2,1)}, u32[]{:S(2)}) copy-start(bf16[192,192]{1,0:T(8,128)(2,1)} %param.28) | copy-start | bytes 221188
  6.5 21.8 %copy-start.3 = (bf16[3,4,1440]{2,1,0:T(4,128)(2,1)S(1)}, bf16[3,4,1440]{2,1,0:T(4,128)(2,1)}, u32[]{:S(2)}) copy-start(bf16[3,4,1440]{2,1,0:T(4,128)(2,1)} %param.15) | copy-start | bytes 103684
  6.5 23.5 %copy-start.8 = (s32[256]{0:T(256)S(1)}, s32[256]{0:T(256)}, u32[]{:S(2)}) copy-start(s32[256]{0:T(256)} %param.19) | copy-start | bytes 3076
  10.9 46.5 %all-to-all-start.2 = ((bf16[128,4,256]{2,1,0:T(4,128)(2,1)}), bf16[128,4,256]{2,1,0:T(4,128)(2,1)S(1)}, u32[]{:S(2)}, u32[]{:S(2)}) async-start(bf16[128,4,256]{2,1,0:T(4,128)(2,1)} %reshape.488), calls=%async_computation.2 | async-start | bytes 524288 | tf_op jit(solution)/shard_map/all_to_all | solution.py:102
  54.7 17.0 %copy-start.2 = (bf16[256,32,64]{0,2,1:T(8,128)(2,1)S(1)}, bf16[256,32,64]{0,2,1:T(8,128)(2,1)}, u32[]{:S(2)}) copy-start(bf16[256,32,64]{0,2,1:T(8,128)(2,1)} %param.17) | copy-start | bytes 3145732
  57.4 31.7 %all-to-all-start = ((bf16[128,4,384]{2,1,0:T(4,128)(2,1)}), bf16[128,4,384]{2,1,0:T(4,128)(2,1)S(1)}, u32[]{:S(2)}, u32[]{:S(2)}) async-start(bf16[128,4,384]{2,1,0:T(4,128)(2,1)} %reshape.482), calls=%async_computation | async-start | bytes 786432 | tf_op jit(solution)/shard_map/all_to_all | solution.py:101
  78.9 17.9 %copy-start.4 = (s32[2,4096]{1,0:T(2,128)S(1)}, s32[2,4096]{1,0:T(2,128)}, u32[]{:S(2)}) copy-start(s32[2,4096]{1,0:T(2,128)} %param.22) | copy-start | bytes 98308
  89.1 59.6 %all-to-all-start.1 = ((bf16[128,4,2048]{2,1,0:T(4,128)(2,1)}), bf16[128,4,2048]{2,1,0:T(4,128)(2,1)}, u32[]{:S(2)}, u32[]{:S(2)}) async-start(bf16[128,4,2048]{2,1,0:T(4,128)(2,1)} %reshape.485), calls=%async_computation.1 | async-start | bytes 4194304 | tf_op jit(solution)/shard_map/all_to_all | solution.py:103
  96.7 146.3 %all-gather.3.cloned.1.call-start = ((), (), s32[]{:S(2)}) async-start(), calls=%async_computation.4 | async-start | bytes 1585152 | tf_op jit(solution)/shard_map/all_gather | solution.py:147
  162.5 3.7 copy-start.10
  162.5 3.7 copy-start.5
  162.6 4.0 copy-start.7
  162.6 4.3 %copy-start.1 = (bf16[48,49]{1,0:T(8,128)(2,1)S(1)}, bf16[48,49]{1,0:T(8,128)(2,1)}, u32[]{:S(2)}) copy-start(bf16[48,49]{1,0:T(8,128)(2,1)} %param.24) | copy-start | bytes 14116
  164.9 93.5 %copy-start.6 = (bf16[12,48]{1,0:T(8,128)(2,1)S(1)}, bf16[12,48]{1,0:T(8,128)(2,1)}, u32[]{:S(2)}) copy-start(bf16[12,48]{1,0:T(8,128)(2,1)} %param.23) | copy-start | bytes 3460
  166.0 186.3 %all-gather.5.cloned.1.call-start = ((), (), s32[]{:S(2)}) async-start(), calls=%async_computation.5 | async-start | bytes 3932160 | tf_op jit(solution)/shard_map/all_gather | solution.py:174
  293.0 18.6 %copy-start.11 = (bf16[192]{0:T(256)(128)(2,1)S(1)}, bf16[192]{0:T(256)(128)(2,1)}, u32[]{:S(2)}) copy-start(bf16[192]{0:T(256)(128)(2,1)} %param.27) | copy-start | bytes 1156
  293.0 59.3 %copy-start.9 = (bf16[192,192]{1,0:T(8,128)(2,1)S(1)}, bf16[192,192]{1,0:T(8,128)(2,1)}, u32[]{:S(2)}) copy-start(bf16[192,192]{1,0:T(8,128)(2,1)} %param.26) | copy-start | bytes 221188
  311.4 91.9 %reduce-scatter.2.cloned.1.call-start = ((), (), s32[]{:S(2)}) async-start(), calls=%async_computation.6 | async-start | bytes 3932160 | tf_op jit(solution)/shard_map/reduce_scatter | solution.py:179
  359.3 0.7 copy-start.12
Sparse Core Ops, SparseCore 0:
  166.1 76.8 all-gather.2
  311.5 40.7 all-gather.4
  359.4 43.8 reduce-scatter.1
where the time goes:
time: 436 us; the launch traced here: 428 us
  waiting for transfers between devices  213 us (49%)
  local copies, waits for them, and re-layouts  68.7 us (16%)
  blocking collectives  44.7 us (10%)
  starting transfers between devices  39.8 us (9%)
  other arithmetic  32.3 us (7%)
  matrix products  15 us (3%)
  between operations  13.8 us (3%)
    all_gather x1, waiting for transfers between devices, body(): piece = lax.all_gather(strips, 'band', axis=0, tiled=True)  75.1 us
    all_to_all x1, waiting for transfers between devices, body(): lax.all_to_all(place_rows(remap_lon), 'band', split_axis=0, concat_axis=0...  48.8 us
    all_gather x1, waiting for transfers between devices, body(): lax.all_gather(normed, 'chan', axis=0, tiled=True)  40.7 us
    reduce_scatter x1, waiting for transfers between devices, body(): lax.psum_scatter(jnp.einsum('hc,hp->cp', columns, activated, preferred_el...  38.4 us
    gather x2, local copies, waits for them, and re-layouts, body(): lax.dynamic_slice(atmos, (zero_index, zero_index, start_col), (local_fiel...  24.7 us
    add x1, other arithmetic, depthwise(): total + weight_col[:, None, None] * flat_rows[:, :, offset:offset + rows...  22.8 us
    all_to_all x1, starting transfers between devices, body(): lax.all_to_all(place_rows(remap_lat), 'band', split_axis=0, concat_axis=0...  17.4 us
    psum x1, blocking collectives, body(): lax.psum(jnp.sum(values * values, axis=0).astype(jnp.bfloat16), 'chan')  17.2 us
  transfers between devices with their start and end apart: 6, of which 5 were waited for; matrix products, arithmetic and copies ran while one was open for 11% of the time, Pallas kernels for 0%

commit v1 on v0

v1 whole, which is shorter than its diff:
```python
import functools

import jax
import jax.numpy as jnp
from jax import lax
from jax.experimental import pallas as pl
from jax.experimental.pallas import tpu as pltpu
from jax.sharding import PartitionSpec as P

MESH = pl.DeviceIdType.MESH
F32 = jnp.float32
BF16 = jnp.bfloat16
NX = 4
CORES = 2


def iota(shape, axis):
    return lax.broadcasted_iota(jnp.int32, shape, axis)


def onehot(mask):
    return jnp.where(mask, 1.0, 0.0).astype(BF16)


def mm(a, b):
    return lax.dot_general(a, b, (((1,), (0,)), ((), ())), preferred_element_type=F32)


def mm_nt(a, b):
    return lax.dot_general(a, b, (((1,), (1,)), ((), ())), preferred_element_type=F32)


def mm_tn(a, b):
    return lax.dot_general(a, b, (((0,), (0,)), ((), ())), preferred_element_type=F32)


def third(v):
    return jnp.where(v >= 6, 2, jnp.where(v >= 3, 1, 0))


def kernel(
    side,
    ints,
    atm,
    lat,
    lon,
    mask,
    stem_w,
    dw_w,
    small,
    w_in,
    w_out,
    out,
    xw,
    pls,
    send,
    recv,
    agg,
    part,
    flux,
    stacked,
    strips,
    gath,
    kmats,
    msgs,
    rb,
    fx,
    dmat,
    smat,
    rowsel,
    yx,
    zbuf,
    shift_all,
    w_all,
    o_all,
    c_loc,
    c_all,
    s_loc,
    s_all,
    sm_all,
    winp,
    bcol,
    vcol,
    hcol,
    res,
    p1_send,
    p1_recv,
    p2_send,
    p2_recv,
    a_send,
    a_recv,
    x_send,
    x_recv,
    b_send,
    b_recv,
    w_send,
    w_recv,
    f_send,
    f_recv,
    loc_sem,
):
    n = side
    group = n * CORES
    band = lax.axis_index("band")
    x = lax.axis_index("chan")
    y = band // group
    zc = lax.rem(band, group)
    z = zc // CORES
    c = lax.rem(zc, CORES)
    mine = (zc, y * CORES + c)
    ring = (y, z)

    def band_at(yy, zz, cc):
        return (yy * n + zz) * CORES + cc

    def group_band(k, idx):
        if k == 0:
            return y * group + idx
        return band_at(idx // CORES, z, lax.rem(idx, CORES))

    def ring_band(k, t):
        return band_at(t, z, c) if k == 0 else band_at(y, t, c)

    def remote(src, dst, ssem, rsem, tb, tx):
        return pltpu.make_async_remote_copy(
            src_ref=src,
            dst_ref=dst,
            send_sem=ssem,
            recv_sem=rsem,
            device_id={"band": tb, "chan": tx},
            device_id_type=MESH,
        )

    barrier = pltpu.get_barrier_semaphore()

    def greet(tb, tx):
        pl.semaphore_signal(
            barrier, inc=1, device_id={"band": tb, "chan": tx}, device_id_type=MESH
        )

    @pl.loop(1, group)
    def _(d):
        greet(y * group + lax.rem(zc + d, group), x)

    @pl.loop(1, n)
    def _(d):
        yy = lax.rem(y + d, n)
        greet(band_at(yy, z, 0), x)
        greet(band_at(yy, z, 1), x)

    @pl.loop(1, NX)
    def _(dx):
        xx = lax.rem(x + dx, NX)
        greet(band, xx)

        @pl.loop(1, n)
        def _(d):
            greet(band_at(lax.rem(y + d, n), z, c), xx)
            greet(band_at(y, lax.rem(z + d, n), c), xx)

    pairs = lon.shape[2]
    tiles = pairs
    owner = ints[0:1, :]
    tile = ints[1:2, :]
    col = ints[2:3, :]
    nq = atm.shape[1]
    quot = col // 32
    shift = lax.rem(col, 32)
    qi = iota((nq, pairs), 0)
    blocks0 = mm(atm[...], onehot(qi == quot)).reshape(32, 16, pairs)
    blocks1 = mm(atm[...], onehot(qi == quot + 1)).reshape(32, 16, pairs)
    rows = [blocks0[i] for i in range(32)] + [blocks1[i] for i in range(32)]
    for bit in (16, 8, 4, 2, 1):
        on = jnp.broadcast_to(lax.rem(shift // bit, 2) == 1, (16, pairs))
        count = len(rows) - bit
        rows = [jnp.where(on, rows[i + bit], rows[i]) for i in range(count)]
    for i in range(32):
        xw[i] = rows[i]

    half = min(128, pairs)
    for ph in range(pairs // half):
        for jb in range(2):

            def step(ci, accs):
                block = lon[ci, jb * 32 : jb * 32 + 32, ph * half : (ph + 1) * half].astype(F32)
                return tuple(
                    accs[fr] + xw[ci, fr : fr + 1, ph * half : (ph + 1) * half] * block
                    for fr in range(12)
                )

            accs = lax.fori_loop(
                0, 32, step, tuple(jnp.zeros((32, half), F32) for _ in range(12)), unroll=4
            )
            for f in range(3):
                for r in range(4):
                    pls[r, f * 64 + jb * 32 : f * 64 + jb * 32 + 32, ph * half : (ph + 1) * half] = (
                        accs[f * 4 + r].astype(BF16)
                    )
    for r in range(4):
        pls[r, 192:256, :] = lat[r]

    ti = iota((tiles, pairs), 0)
    named = onehot(ti == tile)
    owner16 = jnp.broadcast_to(owner, (16, tiles)).astype(F32).astype(BF16)
    place = mm(owner16, named)[0:1, :].astype(jnp.int32)
    same = mm_tn(named, named)
    earlier = iota((pairs, pairs), 0) < iota((pairs, pairs), 1)
    rank = jnp.sum(jnp.where(earlier, same, 0.0), axis=0, keepdims=True).astype(jnp.int32)
    kk = lax.rem(place, 2)
    to_band = place // 2
    to_y = to_band // group
    to_zc = lax.rem(to_band, group)
    to_z = to_zc // CORES
    to_c = lax.rem(to_zc, CORES)
    slot = jnp.where(
        kk == 0,
        (to_zc * n + to_y) * 2 + rank,
        ((group + to_y * CORES + to_c) * n + to_z) * 2 + rank,
    )
    slots = 2 * group * n * 2
    perm = onehot(iota((slots, pairs), 0) == slot)
    for r in range(4):
        send[:, r] = mm_nt(perm, pls[r]).astype(BF16).reshape(2 * group, 2 * n, 256)

    greetings = (group - 1) + 2 * (n - 1) + 3 * (2 * n - 1)
    pl.semaphore_wait(barrier, greetings)

    def p1(k, d):
        idx = lax.rem(mine[k] + d, group)
        return remote(
            send.at[k * group + idx],
            recv.at[k, mine[k]],
            p1_send.at[k, idx],
            p1_recv.at[k, mine[k]],
            group_band(k, idx),
            x,
        )

    def p1_in(k, d):
        idx = lax.rem(mine[k] + d, group)
        return remote(
            send.at[k * group + idx],
            recv.at[k, idx],
            p1_send.at[k, idx],
            p1_recv.at[k, idx],
            group_band(k, idx),
            x,
        )

    @pl.loop(1, group)
    def _(d):
        p1(0, d).start()
        p1(1, d).start()

    for k in range(2):
        recv[k, mine[k]] = send[k * group + mine[k]]

    wide = 49 * 16
    lane = iota((49, wide), 1)
    spread = onehot(iota((49, wide), 0) == lane // 16)
    fields = onehot(iota((12, wide), 0) == lax.rem(iota((12, wide), 1), 16))
    combined = mm(dw_w[...], spread) * mm_tn(stem_w[...], fields)
    c_loc[...] = combined.astype(BF16)
    s_loc[...] = mm_tn(stem_w[...], onehot(iota((12, 16), 0) == iota((12, 16), 1))).astype(BF16)
    shares = ((w_in, w_all), (w_out, o_all), (c_loc, c_all), (s_loc, s_all), (small, sm_all))

    def share(i, dx):
        src, dst = shares[i]
        xx = lax.rem(x + dx, NX)
        return remote(src, dst.at[x], w_send.at[i, dx], w_recv.at[i, x], band, xx)

    def share_in(i, dx):
        src, dst = shares[i]
        xx = lax.rem(x + dx, NX)
        return remote(src, dst.at[xx], w_send.at[i, dx], w_recv.at[i, xx], band, xx)

    for dx in range(1, NX):
        for i in (4, 2, 3, 1, 0):
            share(i, dx).start()
    for src, dst in shares:
        dst[x] = src[...]

    ui = iota((tiles, tiles), 0)
    owner1 = jnp.broadcast_to(owner + 1, (16, tiles)).astype(F32).astype(BF16)
    near_rows = [mm(owner1, onehot(ui == ints[3 + s : 4 + s, :]))[0:1, :] for s in range(4)]
    near = jnp.concatenate(near_rows + [jnp.zeros((12, tiles), F32)], axis=0).astype(BF16)
    near_at = mm_nt(near, onehot(ui == owner)).astype(BF16)
    mrows = n * NX * 16
    mcols = group * 32
    mr = iota((mrows, tiles), 0)
    mt, mx, mrho = mr // 64, lax.rem(mr // 16, NX), lax.rem(mr, 16)
    ci = iota((mrows, mcols), 1)
    rho = lax.rem(iota((mrows, mcols), 0), 16)
    to_h = lax.rem(iota((mrows, mcols), 0) // 16, 2)
    src, src_half, src_rho = ci // 32, lax.rem(ci // 16, 2), lax.rem(ci, 16)
    for k in range(2):
        to_place = 2 * (ring_band(k, mt)) + mx // 2
        cols = mm_nt(onehot(iota((mrows, tiles), 1) == to_place), near_at).astype(jnp.int32)
        if k == 0:
            src_place = 2 * (y * group + src)
        else:
            src_place = 2 * band_at(src // CORES, z, lax.rem(src, CORES)) + 1
        src_tag = jnp.where(src_rho == rho, src_place + 1, -1)
        col_ns = jnp.where(to_h == 0, cols[:, 0:1], cols[:, 1:2])
        col_we = jnp.where(rho < 9, cols[:, 2:3], cols[:, 3:4])
        half_we = jnp.where(rho < 9, 0, 1)
        kmats[k, 0] = onehot((col_ns == src_tag) & (src_half == to_h))
        kmats[k, 1] = onehot((col_we == src_tag) & (src_half == half_we))

    h = lax.rem(x, 2)
    frows = 38 * 16
    fr_row = iota((frows, 640), 0)
    r_row, f_row = fr_row // 16, lax.rem(fr_row, 16)
    fx_row = f_row // 3
    fl_row = f_row - 3 * fx_row
    strip_a = jnp.where(h == 0, r_row, r_row - 35)
    in_strip = (strip_a >= 0) & (strip_a <= 2)
    want = jnp.where(
        in_strip,
        576 + fx_row * 16 + fl_row * 3 + strip_a,
        f_row * 48 + jnp.where(h == 0, r_row - 3, r_row + 13),
    )
    smat[...] = onehot((want == iota((frows, 640), 1)) & (f_row < 12))
    rr = iota((frows, 128), 0) // 16
    ff = lax.rem(iota((frows, 128), 0), 16)
    ll = iota((frows, 128), 1)
    cell = rr - 3 + 32 * h
    rowsel[0] = onehot((cell == lax.rem(ll, 64)) & (cell >= 0) & (cell < 64))
    lo = ll < 64
    lx, lrho = lax.rem(ll, 64) // 16, lax.rem(ll, 16)
    fa = jnp.where(lo, lrho - 9, jnp.where(lrho < 9, lrho, lrho - 2))
    ok = (lo & (lrho >= 9)) | (jnp.logical_not(lo) & (lrho < 11))
    rowsel[1] = onehot(ok & (3 * lx + third(fa) == ff))
    kr = iota((128, 128), 0)
    klo = kr < 64
    krho = lax.rem(kr, 16)
    kfa = jnp.where(klo, krho - 9, jnp.where(krho < 9, krho, krho - 2))
    kwest = jnp.logical_not(klo) & (krho < 9)
    lane_to = jnp.where(kwest, 64, 67) + kfa - 3 * third(kfa)
    collapse = onehot(lane_to == iota((128, 128), 1))
    ar = iota((256, 896), 0)
    al = lax.rem(ar, 128)
    ncol = jnp.where(al < 64, al + 3, jnp.where(al < 67, al - 64, jnp.where(al < 70, al, -999)))
    bc = iota((256, 896), 1)
    shift_all[...] = onehot(
        (ar // 128 == lax.rem(bc, 128) // 64) & (ncol == lax.rem(bc, 64) + bc // 128)
    )
    dmat[...] = jnp.zeros(dmat.shape, BF16)
    sr = iota((32, 192), 0)
    sl = iota((32, 192), 1)
    srho = lax.rem(sr, 16)
    sfl = third(srho)
    sa = srho - 3 * sfl
    pick_rows = onehot(
        (srho < 9) & (sl // 64 == sfl) & (lax.rem(sl, 64) == sa + jnp.where(sr < 16, 61, 0))
    )
    er = iota((48, 192), 0)
    el = iota((48, 192), 1)
    erho = lax.rem(er, 16)
    efa = jnp.where(er < 16, erho, jnp.where(er < 32, erho - 9, erho - 2))
    eok = (
        ((er < 16) & (erho < 9))
        | ((er >= 16) & (er < 32) & (erho >= 9))
        | ((er >= 32) & (erho >= 9) & (erho < 11))
    )
    efl = third(efa)
    ea = efa - 3 * efl + jnp.where(er < 16, 61, 0)
    pick_cols = onehot(eok & (el // 64 == efl) & (lax.rem(el, 64) == ea))

    def p2(k, d):
        t = lax.rem(ring[k] + d, n)
        return remote(
            agg.at[k, t],
            part.at[k, ring[k]],
            p2_send.at[k, t],
            p2_recv.at[k, ring[k]],
            ring_band(k, t),
            x,
        )

    def p2_in(k, d):
        t = lax.rem(ring[k] + d, n)
        return remote(
            agg.at[k, t],
            part.at[k, t],
            p2_send.at[k, t],
            p2_recv.at[k, t],
            ring_band(k, t),
            x,
        )

    krows = group * 8 * n
    k_tile = lax.rem(iota((64, krows), 1) // 2, n)
    for k in range(2):

        @pl.loop(1, group)
        def _(d):
            p1_in(k, d).wait_recv()

        got = recv[k].reshape(krows, 256)
        lat_t = got[:, 128:256].astype(F32).T[64:128, :]
        lhs = jnp.concatenate(
            [jnp.where(k_tile == t, lat_t, 0.0).astype(BF16) for t in range(n)], axis=0
        )
        agg[k] = mm(lhs, got[:, 0:192]).astype(BF16).reshape(n, 64, 192)

        @pl.loop(1, n)
        def _(d):
            p2(k, d).start()

        part[k, ring[k]] = agg[k, ring[k]]

    for dx in range(1, NX):
        for i in range(5):
            share_in(i, dx).wait_recv()
    gains = jnp.zeros((16, 192), F32)
    for i in range(NX):
        put = onehot(iota((256, 192), 1) == jnp.where(iota((256, 192), 0) < 48, iota((256, 192), 0) + 48 * i, -1))
        gains = gains + mm(sm_all[i], put)
    row2 = onehot(iota((16, 128), 0) == 2)
    row0 = onehot(iota((16, 128), 0) == 0)
    head = mm_tn(gains.astype(BF16), row2)
    hcol[...] = head
    for i in range(NX):
        blk = pl.ds(i * 192, 192)
        winp[blk, :] = (w_all[i].astype(F32) * gains[1:2, :]).astype(BF16)
        bcol[blk, :] = mm_tn(sm_all[i, :, 0:192], row0)
        vcol[blk, :] = 0.5 * mm(o_all[i], head.astype(BF16))

    def xcopy(dx):
        xx = lax.rem(x + dx, NX)
        at = pl.multiple_of(16 * lax.rem(xx, 2), 16)
        return remote(
            flux.at[xx // 2, pl.ds(at, 48)], fx.at[x], x_send.at[dx], x_recv.at[x], band, xx
        )

    def xcopy_in(dx):
        xx = lax.rem(x + dx, NX)
        at = pl.multiple_of(16 * lax.rem(xx, 2), 16)
        return remote(
            flux.at[xx // 2, pl.ds(at, 48)], fx.at[xx], x_send.at[dx], x_recv.at[xx], band, xx
        )

    def acopy(k, d):
        idx = lax.rem(mine[k] + d, group)
        return remote(
            strips.at[k],
            gath.at[k, mine[k]],
            a_send.at[k, idx],
            a_recv.at[k, mine[k]],
            group_band(k, idx),
            x,
        )

    def acopy_in(k, d):
        idx = lax.rem(mine[k] + d, group)
        return remote(
            strips.at[k],
            gath.at[k, idx],
            a_send.at[k, idx],
            a_recv.at[k, idx],
            group_band(k, idx),
            x,
        )

    for k in range(2):

        @pl.loop(1, n)
        def _(d):
            p2_in(k, d).wait_recv()

        total = jnp.zeros((64, 192), F32)
        for t in range(n):
            total = total + part[k, t].astype(F32)
        tile_flux = (total * mask[k]).astype(BF16)
        flux[k] = tile_flux
        for f in range(3):
            stacked[f * 64 : f * 64 + 64, :] = tile_flux[:, f * 64 : f * 64 + 64]
        ns = mm(pick_rows, stacked[...])
        we = mm_nt(pick_cols, tile_flux)
        strips[k, 0:16, :] = jnp.concatenate([ns[0:16], we[0:16]], axis=1).astype(BF16)
        strips[k, 16:32, :] = jnp.concatenate([ns[16:32] + we[16:32], we[32:48]], axis=1).astype(
            BF16
        )

        @pl.loop(1, group)
        def _(d):
            acopy(k, d).start()

        gath[k, mine[k]] = strips[k]

    for dx in range(1, NX):
        xcopy(dx).start()
    fx[x] = flux[x // 2, pl.ds(pl.multiple_of(16 * h, 16), 48), :]

    def bcopy(k, t, xx):
        return remote(
            msgs.at[k, t, xx],
            rb.at[k, x, ring[k]],
            b_send.at[k, t, xx],
            b_recv.at[k, x, ring[k]],
            ring_band(k, t),
            xx,
        )

    def bcopy_in(k, t, xx):
        return remote(
            msgs.at[k, t, xx],
            rb.at[k, xx, t],
            b_send.at[k, t, xx],
            b_recv.at[k, xx, t],
            ring_band(k, t),
            xx,
        )

    def each_b(k, fn):
        @pl.loop(1, NX)
        def _(dx):
            fn(k, ring[k], lax.rem(x + dx, NX))

        @pl.loop(1, n)
        def _(d):
            for dx in range(NX):
                fn(k, lax.rem(ring[k] + d, n), lax.rem(x + dx, NX))

    low = iota((mrows, 128), 1) < 64
    body_rows = lax.rem(iota((mrows, 128), 0), 16) < 9
    for k in range(2):

        @pl.loop(1, group)
        def _(d):
            acopy_in(k, d).wait_recv()

        flat = gath[k].reshape(mcols, 128)
        msg = jnp.where(low & body_rows, mm(kmats[k, 0], flat), mm(kmats[k, 1], flat))
        msgs[k] = msg.astype(BF16).reshape(n, NX, 16, 128)
        each_b(k, lambda k, t, xx: bcopy(k, t, xx).start())
        rb[k, x, ring[k]] = msgs[k, ring[k], x]

    for dx in range(1, NX):
        xcopy_in(dx).wait_recv()
    for f in range(12):
        dmat[f * 48 : f * 48 + 48, 0:64] = fx[f // 3, :, (f % 3) * 64 : (f % 3) * 64 + 64]
    for k in range(2):
        each_b(k, lambda k, t, xx: bcopy_in(k, t, xx).wait_recv())
    total = jnp.zeros((NX, 16, 128), F32)
    for k in range(2):
        for t in range(n):
            total = total + rb[k, :, t].astype(F32)
    edge = total.reshape(64, 128)
    dmat[576:640, 0:64] = edge[:, 0:64].astype(BF16)
    elow = iota((64, 128), 1) < 64
    both = jnp.concatenate([jnp.where(elow, edge, 0.0), jnp.where(elow, 0.0, edge)], axis=0)
    picked = mm_nt(rowsel[0], both.astype(BF16)) * rowsel[1].astype(F32)
    yx[...] = (mm(smat[...], dmat[...]) + mm(picked.astype(BF16), collapse)).astype(BF16)
    pair_rows = jnp.concatenate([yx[0:592, :], yx[16:608, :]], axis=1)
    for b in range(7):
        zbuf[:, b] = (
            mm(pair_rows, shift_all[:, b * 128 : b * 128 + 128]).astype(BF16).reshape(37, 16, 128)
        )

    @pl.loop(0, 8)
    def _(i):
        left = zbuf[pl.ds(4 * i, 7)].reshape(wide, 128)
        right = zbuf[pl.ds(4 * i + 2, 7)].reshape(wide, 128)
        mixed = mm(c_all[...].reshape(192, wide), jnp.concatenate([left, right], axis=1))
        mean = jnp.sum(mixed, axis=0, keepdims=True) * (1.0 / 192.0)
        sq = jnp.sum(mixed * mixed, axis=0, keepdims=True) * (1.0 / 192.0)
        scale = lax.rsqrt(sq - mean * mean + 1e-06)
        normed = ((mixed - mean) * scale).astype(BF16)
        centre = jnp.concatenate([zbuf[4 * i + 3, 3], zbuf[4 * i + 5, 3]], axis=1)
        inner = mm(s_all[...].reshape(192, 16), centre).astype(BF16).astype(F32)
        hc = jnp.concatenate([hcol[...], hcol[...]], axis=1)
        acc = jnp.sum(inner * hc, axis=0, keepdims=True)
        for q in range(6):
            blk = slice(q * 128, q * 128 + 128)
            bias = jnp.concatenate([bcol[blk, :], bcol[blk, :]], axis=1)
            vals = jnp.concatenate([vcol[blk, :], vcol[blk, :]], axis=1)
            pre = mm(winp[blk, :], normed) + bias
            inside = pre * (0.7978845608 + (0.7978845608 * 0.044715) * (pre * pre))
            acc = acc + jnp.sum(vals * (pre * (1.0 + jnp.tanh(inside))), axis=0, keepdims=True)
        res[i] = acc

    out[x] = jnp.concatenate([res[i] for i in range(8)], axis=0)

    def fcopy(dx):
        xx = lax.rem(x + dx, NX)
        return remote(out.at[x], out.at[x], f_send.at[dx], f_recv.at[x], band, xx)

    def fcopy_in(dx):
        xx = lax.rem(x + dx, NX)
        return remote(out.at[x], out.at[xx], f_send.at[dx], f_recv.at[xx], band, xx)

    for dx in range(1, NX):
        fcopy(dx).start()

    for k in range(2):

        @pl.loop(1, group)
        def _(d):
            p1(k, d).wait_send()
            acopy(k, d).wait_send()

        @pl.loop(1, n)
        def _(d):
            p2(k, d).wait_send()

        each_b(k, lambda k, t, xx: bcopy(k, t, xx).wait_send())
    for dx in range(1, NX):
        xcopy(dx).wait_send()
        for i in range(5):
            share(i, dx).wait_send()
    for dx in range(1, NX):
        fcopy(dx).wait_send()
        fcopy_in(dx).wait_recv()


def body(
    side,
    atmos,
    remap_lat,
    remap_lon,
    pair_tile,
    pair_col,
    tile_owner,
    neighbours,
    land_mask,
    stem_w,
    dw_w,
    ln_gain,
    w_in,
    b_in,
    w_out,
    head_w,
):
    n = side
    group = n * CORES
    pairs = pair_col.shape[0]
    ints = jnp.concatenate(
        [tile_owner[None], pair_tile.T, pair_col[None], neighbours.T, tile_owner[None]], axis=0
    )
    atm = atmos.reshape(12, 45, 32).transpose(2, 0, 1)
    atm = jnp.pad(atm, ((0, 0), (0, 4), (0, 3))).reshape(512, 48)
    lat = remap_lat.transpose(2, 1, 0)
    lon = remap_lon.transpose(1, 2, 0)
    mask = jnp.tile(land_mask.reshape(2, 64, 64), (1, 1, 3)).astype(F32)
    small = jnp.stack(
        [jnp.pad(b_in, (0, 64)), jnp.pad(ln_gain, (0, 208)), jnp.pad(head_w, (0, 208))]
    )
    small = jnp.pad(small, ((0, 13), (0, 0)))
    vmem = pltpu.VMEM
    dma = pltpu.SemaphoreType.DMA
    frows = 38 * 16
    result = pl.pallas_call(
        functools.partial(kernel, n),
        out_shape=jax.ShapeDtypeStruct((NX, 8, 256), F32),
        in_specs=[pl.BlockSpec(memory_space=vmem)] * 10,
        out_specs=pl.BlockSpec(memory_space=vmem),
        scratch_shapes=[
            vmem((32, 16, pairs), F32),
            vmem((4, 256, pairs), BF16),
            vmem((2 * group, 4, 2 * n, 256), BF16),
            vmem((2, group, 4, 2 * n, 256), BF16),
            vmem((2, n, 64, 192), BF16),
            vmem((2, n, 64, 192), BF16),
            vmem((2, 64, 192), BF16),
            vmem((192, 64), BF16),
            vmem((2, 32, 128), BF16),
            vmem((2, group, 32, 128), BF16),
            vmem((2, 2, n * NX * 16, group * 32), BF16),
            vmem((2, n, NX, 16, 128), BF16),
            vmem((2, NX, n, 16, 128), BF16),
            vmem((NX, 48, 192), BF16),
            vmem((640, 128), BF16),
            vmem((frows, 640), BF16),
            vmem((2, frows, 128), BF16),
            vmem((frows, 128), BF16),
            vmem((37, 7, 16, 128), BF16),
            vmem((256, 896), BF16),
            vmem((NX, 192, 192), BF16),
            vmem((NX, 192, 192), BF16),
            vmem((48, 784), BF16),
            vmem((NX, 48, 784), BF16),
            vmem((48, 16), BF16),
            vmem((NX, 48, 16), BF16),
            vmem((NX, 16, 256), BF16),
            vmem((768, 192), BF16),
            vmem((768, 128), F32),
            vmem((768, 128), F32),
            vmem((192, 128), F32),
            vmem((8, 1, 256), F32),
            dma((2, group)),
            dma((2, group)),
            dma((2, n)),
            dma((2, n)),
            dma((2, group)),
            dma((2, group)),
            dma((NX,)),
            dma((NX,)),
            dma((2, n, NX)),
            dma((2, NX, n)),
            dma((5, NX)),
            dma((5, NX)),
            dma((NX,)),
            dma((NX,)),
            dma((1,)),
        ],
        compiler_params=pltpu.CompilerParams(
            collective_id=0, has_side_effects=True, vmem_limit_bytes=56 * 1024 * 1024
        ),
        cost_estimate=pl.CostEstimate(flops=4000000000, bytes_accessed=4000000, transcendentals=2000000),
    )(ints, atm, lat, lon, mask, stem_w, dw_w, small, w_in, w_out)
    return result.reshape(2, 4096) * land_mask.astype(F32)


def solution(mesh):
    side = 1
    while side * side * CORES < mesh.shape["band"]:
        side *= 2
    return jax.shard_map(
        functools.partial(body, side),
        mesh=mesh,
        in_specs=(
            P("chan", "band", None),
            P("band", None, None),
            P("band", None, None),
            P("band", None),
            P("band"),
            P(),
            P(),
            P("band", None),
            P(None, "chan"),
            P("chan", None),
            P("chan"),
            P("chan", None),
            P("chan"),
            P("chan", None),
            P("chan"),
        ),
        out_specs=P("band", None),
        check_vma=False,
    )
```

time: 436 us -> 80.3 us (0.18)
  the two profiles are of different devices: /device:TPU:8 before, /device:TPU:1 now
where the time goes in v1:
time: 80.3 us; the launch traced here: 79.8 us
  Pallas kernels  70.8 us (88%)
  local copies, waits for them, and re-layouts  6.97 us (9%)
  other arithmetic  2.01 us (3%)
    pallas_call x1, Pallas kernels, body(): pl.pallas_call(functools.partial(kernel, n), out_shape=jax.ShapeDtypeStru...  70.8 us
    unnamed x22, local copies, waits for them, and re-layouts  3.75 us

profile of v1, /device:TPU:1, one launch (start us, length us, event | category | flops | bytes accessed | tf_op | source)
XLA Modules:
  0.0 79.8 jit_solution(15693256024676774955)
XLA Ops:
  0.0 0.8 convert_element_type.17
  0.8 0.1 convert_element_type.18
  0.9 0.1 copy.20
  1.0 0.0 copy-start.2
  1.0 0.8 copy.21.mask
  1.8 0.0 copy-done.2
  1.8 0.1 reshape.15
  1.9 0.2 copy.22
  2.1 0.0 copy-start.1
  2.1 0.7 pad.19.clone
  2.8 0.2 copy-done.1
  3.0 0.7 copy.24
  3.7 0.0 copy-start.7
  3.7 0.7 copy-done.7
  4.4 0.0 copy-start.8
  4.4 0.6 copy-done.8
  5.0 0.0 copy-start.9
  5.0 0.6 copy-done.9
  5.7 0.0 copy-start.5
  5.7 0.0 copy-start.6
  5.7 0.6 fusion.4.small
  6.3 0.0 copy-start.4
  6.3 0.0 copy-done.5
  6.4 0.0 copy-done.6
  6.4 0.6 copy-done.4
  7.0 0.0 copy-done.3
  7.0 0.6 concatenate.3.ints
  7.6 70.8 %shard_map.145 = f32[4,8,256]{2,1,0:T(8,128)} custom-call(s32[8,256]{1,0:T(8,128)} %concatenate.3.ints, bf16[512,48]{1,0:T(8,128)(2,1)} %bitcast.13, bf16[4,64,256]{2,1,0:T(8,128)(2,1)} %bitcast.14, bf16[32,64,256]{2,1,0:T(8,128)(2,1)} %bitcast.20, f32[2,64,192]{2,1,0:T(8,128)} %copy.21.mask, bf16[12,48]{1,0:T(8,128)(2,1)} %stem_w.1, bf16[48,49]{1,0:T(8,128)(2,1)} %dw_w.1, ...), custom_call_target="tpu_custom_call" | custom-call | flops 4000000000 | bytes 4000000 | tf_op jit(solution)/shard_map/pallas_call | solution.py:654
  78.4 0.0 copy-start
  78.4 0.8 reshape.17
  79.2 0.0 copy-done
  79.2 0.6 convert_multiply_fusion
  (8 shorter events, 0.0 us)
Async XLA Ops:
  1.0 0.8 copy-start.2
  2.1 0.9 %copy-start.1 = (bf16[256,64,4]{0,2,1:T(4,128)(2,1)S(1)}, bf16[256,64,4]{0,2,1:T(4,128)(2,1)}, u32[]{:S(2)}) copy-start(bf16[256,64,4]{0,2,1:T(4,128)(2,1)} %param.16) | copy-start | bytes 393220
  3.7 0.7 copy-start.7
  4.4 0.7 copy-start.8
  5.0 0.7 copy-start.9
  5.7 0.7 copy-start.5
  5.7 0.7 copy-start.6
  6.3 0.7 copy-start.4
  6.3 0.7 copy-start.3
  78.4 0.8 %copy-start = (s32[2,4096]{1,0:T(2,128)S(1)}, s32[2,4096]{1,0:T(2,128)}, u32[]{:S(2)}) copy-start(s32[2,4096]{1,0:T(2,128)} %param.22) | copy-start | bytes 98308

commit v2 on v1

--- a/solution.py
+++ b/solution.py
@@ -40,17 +40,45 @@
 
 def kernel(
     side,
-    ints,
+    owner_hbm,
+    tile_hbm,
+    col_hbm,
+    near_hbm,
+    atm_hbm,
+    lon_hbm,
+    lat_hbm,
+    stem_hbm,
+    dw_hbm,
+    b_in_hbm,
+    gain_hbm,
+    head_hbm,
+    w_in_hbm,
+    w_out_hbm,
+    mask_hbm,
+    out,
+    owner_ref,
+    tile_ref,
+    col_ref,
+    near_ref,
     atm,
+    lon,
     lat,
-    lon,
-    mask,
     stem_w,
     dw_w,
-    small,
+    b_in,
+    ln_gain,
+    head_w,
     w_in,
     w_out,
-    out,
+    mask_ref,
+    in_sems,
+    arow,
+    ashift,
+    small_f,
+    small,
+    mrows_ref,
+    mask,
+    got_out,
     xw,
     pls,
     send,
@@ -131,6 +159,31 @@
             device_id_type=MESH,
         )
 
+    loads = [
+        pltpu.make_async_copy(src, dst, in_sems.at[i])
+        for i, (src, dst) in enumerate(
+            (
+                (owner_hbm, owner_ref),
+                (tile_hbm, tile_ref),
+                (col_hbm, col_ref),
+                (near_hbm, near_ref),
+                (atm_hbm, atm),
+                (lon_hbm, lon),
+                (lat_hbm, lat),
+                (stem_hbm, stem_w),
+                (dw_hbm, dw_w),
+                (b_in_hbm, b_in),
+                (gain_hbm, ln_gain),
+                (head_hbm, head_w),
+                (w_in_hbm, w_in),
+                (w_out_hbm, w_out),
+                (mask_hbm, mask_ref),
+            )
+        )
+    ]
+    for load in loads:
+        load.start()
+
     barrier = pltpu.get_barrier_semaphore()
 
     def greet(tb, tx):
@@ -160,22 +213,24 @@
 
     pairs = lon.shape[2]
     tiles = pairs
-    owner = ints[0:1, :]
-    tile = ints[1:2, :]
-    col = ints[2:3, :]
-    nq = atm.shape[1]
-    quot = col // 32
-    shift = lax.rem(col, 32)
-    qi = iota((nq, pairs), 0)
-    blocks0 = mm(atm[...], onehot(qi == quot)).reshape(32, 16, pairs)
-    blocks1 = mm(atm[...], onehot(qi == quot + 1)).reshape(32, 16, pairs)
-    rows = [blocks0[i] for i in range(32)] + [blocks1[i] for i in range(32)]
-    for bit in (16, 8, 4, 2, 1):
-        on = jnp.broadcast_to(lax.rem(shift // bit, 2) == 1, (16, pairs))
-        count = len(rows) - bit
-        rows = [jnp.where(on, rows[i + bit], rows[i]) for i in range(count)]
+    lons = atm.shape[2]
+    padded = arow.shape[1]
+    arow[...] = jnp.zeros(arow.shape, F32)
+    for i in range(5):
+        loads[i].wait()
+    for f in range(3):
+        arow[4 * f : 4 * f + 4, 0:lons] = atm[f].astype(F32)
+    row = arow[...]
     for i in range(32):
-        xw[i] = rows[i]
+        moved = row if i == 0 else pltpu.roll(row, padded - i, 1)
+        ashift[16 * i : 16 * i + 16, :] = moved.astype(BF16)
+    owner = owner_ref[...]
+    tile = tile_ref[...]
+    col = col_ref[...]
+    at_col = onehot(iota((padded, pairs), 0) == col)
+    xw[...] = mm(ashift[...], at_col).reshape(32, 16, pairs)
+    loads[5].wait()
+    loads[6].wait()
 
     half = min(128, pairs)
     for ph in range(pairs // half):
@@ -197,7 +252,7 @@
                         accs[f * 4 + r].astype(BF16)
                     )
     for r in range(4):
-        pls[r, 192:256, :] = lat[r]
+        pls[r, 192:256, :] = lat[:, r, :]
 
     ti = iota((tiles, pairs), 0)
     named = onehot(ti == tile)
@@ -255,6 +310,13 @@
     for k in range(2):
         recv[k, mine[k]] = send[k * group + mine[k]]
 
+    for i in range(7, 15):
+        loads[i].wait()
+    small_f[...] = jnp.zeros(small_f.shape, F32)
+    small_f[0:1, 0:192] = b_in[...].astype(F32)
+    small_f[1:2, 0:48] = ln_gain[...].astype(F32)
+    small_f[2:3, 0:48] = head_w[...].astype(F32)
+    small[...] = small_f[...].astype(BF16)
     wide = 49 * 16
     lane = iota((49, wide), 1)
     spread = onehot(iota((49, wide), 0) == lane // 16)
@@ -282,7 +344,7 @@
 
     ui = iota((tiles, tiles), 0)
     owner1 = jnp.broadcast_to(owner + 1, (16, tiles)).astype(F32).astype(BF16)
-    near_rows = [mm(owner1, onehot(ui == ints[3 + s : 4 + s, :]))[0:1, :] for s in range(4)]
+    near_rows = [mm(owner1, onehot(ui == near_ref[s : s + 1, :]))[0:1, :] for s in range(4)]
     near = jnp.concatenate(near_rows + [jnp.zeros((12, tiles), F32)], axis=0).astype(BF16)
     near_at = mm_nt(near, onehot(ui == owner)).astype(BF16)
     mrows = n * NX * 16
@@ -306,6 +368,16 @@
         half_we = jnp.where(rho < 9, 0, 1)
         kmats[k, 0] = onehot((col_ns == src_tag) & (src_half == to_h))
         kmats[k, 1] = onehot((col_we == src_tag) & (src_half == half_we))
+
+    for k in range(2):
+        for i in range(32):
+            mrows_ref[k, i : i + 1, :] = mask_ref[k : k + 1, 128 * i : 128 * i + 128].astype(F32)
+        mpick = onehot(iota((64, 32), 1) == iota((64, 32), 0) // 2)
+        mfull = mm(mpick, mrows_ref[k].astype(BF16))
+        mswap = pltpu.roll(mfull, 64, 1)
+        meven = lax.rem(iota((64, 128), 0), 2) * 64 + iota((64, 128), 1)
+        keep = (meven < 64) | (meven >= 128)
+        mask[k] = jnp.where(keep, mfull, mswap)
 
     h = lax.rem(x, 2)
     frows = 38 * 16
@@ -402,13 +474,128 @@
         lhs = jnp.concatenate(
             [jnp.where(k_tile == t, lat_t, 0.0).astype(BF16) for t in range(n)], axis=0
         )
-        agg[k] = mm(lhs, got[:, 0:192]).astype(BF16).reshape(n, 64, 192)
+        sums = mm(lhs, got[:, 0:192])
+        agg[k, :, 0:64, :] = sums[:, 0:128].astype(BF16).reshape(n, 64, 128)
+        last = sums[:, 128:192].reshape(n, 2, 32, 64)
+        agg[k, :, 64:96, :] = jnp.concatenate([last[:, 0], last[:, 1]], axis=2).astype(BF16)
 
         @pl.loop(1, n)
         def _(d):
             p2(k, d).start()
 
         part[k, ring[k]] = agg[k, ring[k]]
+
+    def xcopy(dx):
+        xx = lax.rem(x + dx, NX)
+        at = pl.multiple_of(16 * lax.rem(xx, 2), 16)
+        return remote(
+            flux.at[xx // 2, pl.ds(at, 48)], fx.at[x], x_send.at[dx], x_recv.at[x], band, xx
+        )
+
+    def xcopy_in(dx):
+        xx = lax.rem(x + dx, NX)
+        at = pl.multiple_of(16 * lax.rem(xx, 2), 16)
+        return remote(
+            flux.at[xx // 2, pl.ds(at, 48)], fx.at[xx], x_send.at[dx], x_recv.at[xx], band, xx
+        )
+
+    def acopy(k, d):
+        idx = lax.rem(mine[k] + d, group)
+        return remote(
+            strips.at[k],
+            gath.at[k, mine[k]],
+            a_send.at[k, idx],
+            a_recv.at[k, mine[k]],
+            group_band(k, idx),
+            x,
+        )
+
+    def acopy_in(k, d):
+        idx = lax.rem(mine[k] + d, group)
+        return remote(
+            strips.at[k],
+            gath.at[k, idx],
+            a_send.at[k, idx],
+            a_recv.at[k, idx],
+            group_band(k, idx),
+            x,
+        )
+
+    for k in range(2):
+
+        @pl.loop(1, n)
+        def _(d):
+            p2_in(k, d).wait_recv()
+
+        total = part[k, 0].astype(F32)
+        for t in range(1, n):
+            total = total + part[k, t].astype(F32)
+        last = jnp.concatenate([total[64:96, 0:64], total[64:96, 64:128]], axis=0)
+        masked = [total[0:64, :] * mask[k], last * mask[k, :, 0:64]]
+        tile_flux = jnp.concatenate(masked, axis=1).astype(BF16)
+        flux[k] = tile_flux
+        for f in range(3):
+            stacked[f * 64 : f * 64 + 64, :] = tile_flux[:, f * 64 : f * 64 + 64]
+        ns = mm(pick_rows, stacked[...])
+        we = mm_nt(pick_cols, tile_flux)
+        strips[k, 0:16, :] = jnp.concatenate([ns[0:16], we[0:16]], axis=1).astype(BF16)
+        strips[k, 16:32, :] = jnp.concatenate([ns[16:32] + we[16:32], we[32:48]], axis=1).astype(
+            BF16
+        )
+
+        @pl.loop(1, group)
+        def _(d):
+            acopy(k, d).start()
+
+        gath[k, mine[k]] = strips[k]
+
+    for dx in range(1, NX):
+        xcopy(dx).start()
+    fx[x] = flux[x // 2, pl.ds(pl.multiple_of(16 * h, 16), 48), :]
+
+    def bcopy(k, t, xx):
+        return remote(
+            msgs.at[k, t, xx],
+            rb.at[k, x, ring[k]],
+            b_send.at[k, t, xx],
+            b_recv.at[k, x, ring[k]],
+            ring_band(k, t),
+            xx,
+        )
+
+    def bcopy_in(k, t, xx):
+        return remote(
+            msgs.at[k, t, xx],
+            rb.at[k, xx, t],
+            b_send.at[k, t, xx],
+            b_recv.at[k, xx, t],
+            ring_band(k, t),
+            xx,
+        )
+
+    def each_b(k, fn):
+        @pl.loop(1, NX)
+        def _(dx):
+            fn(k, ring[k], lax.rem(x + dx, NX))
+
+        @pl.loop(1, n)
+        def _(d):
+            for dx in range(NX):
+                fn(k, lax.rem(ring[k] + d, n), lax.rem(x + dx, NX))
+
+    low = iota((mrows, 128), 1) < 64
+    body_rows = lax.rem(iota((mrows, 128), 0), 16) < 9
+    for k in range(2):
+
+        @pl.loop(1, group)
+        def _(d):
+            acopy_in(k, d).wait_recv()
+
+        flat = gath[k].reshape(mcols, 128)
+        msg = jnp.where(low & body_rows, mm(kmats[k, 0], flat), mm(kmats[k, 1], flat))
+        msgs[k] = msg.astype(BF16).reshape(n, NX, 16, 128)
+        each_b(k, lambda k, t, xx: bcopy(k, t, xx).start())
+        rb[k, x, ring[k]] = msgs[k, ring[k], x]
 
     for dx in range(1, NX):
         for i in range(5):
@@ -427,116 +614,6 @@
         bcol[blk, :] = mm_tn(sm_all[i, :, 0:192], row0)
         vcol[blk, :] = 0.5 * mm(o_all[i], head.astype(BF16))
 
-    def xcopy(dx):
-        xx = lax.rem(x + dx, NX)
-        at = pl.multiple_of(16 * lax.rem(xx, 2), 16)
-        return remote(
-            flux.at[xx // 2, pl.ds(at, 48)], fx.at[x], x_send.at[dx], x_recv.at[x], band, xx
-        )
-
-    def xcopy_in(dx):
-        xx = lax.rem(x + dx, NX)
-        at = pl.multiple_of(16 * lax.rem(xx, 2), 16)
-        return remote(
-            flux.at[xx // 2, pl.ds(at, 48)], fx.at[xx], x_send.at[dx], x_recv.at[xx], band, xx
-        )
-
-    def acopy(k, d):
-        idx = lax.rem(mine[k] + d, group)
-        return remote(
-            strips.at[k],
-            gath.at[k, mine[k]],
-            a_send.at[k, idx],
-            a_recv.at[k, mine[k]],
-            group_band(k, idx),
-            x,
-        )
-
-    def acopy_in(k, d):
-        idx = lax.rem(mine[k] + d, group)
-        return remote(
-            strips.at[k],
-            gath.at[k, idx],
-            a_send.at[k, idx],
-            a_recv.at[k, idx],
-            group_band(k, idx),
-            x,
-        )
-
-    for k in range(2):
-
-        @pl.loop(1, n)
-        def _(d):
-            p2_in(k, d).wait_recv()
-
-        total = jnp.zeros((64, 192), F32)
-        for t in range(n):
-            total = total + part[k, t].astype(F32)
-        tile_flux = (total * mask[k]).astype(BF16)
-        flux[k] = tile_flux
-        for f in range(3):
-            stacked[f * 64 : f * 64 + 64, :] = tile_flux[:, f * 64 : f * 64 + 64]
-        ns = mm(pick_rows, stacked[...])
-        we = mm_nt(pick_cols, tile_flux)
-        strips[k, 0:16, :] = jnp.concatenate([ns[0:16], we[0:16]], axis=1).astype(BF16)
-        strips[k, 16:32, :] = jnp.concatenate([ns[16:32] + we[16:32], we[32:48]], axis=1).astype(
-            BF16
-        )
-
-        @pl.loop(1, group)
-        def _(d):
-            acopy(k, d).start()
-
-        gath[k, mine[k]] = strips[k]
-
-    for dx in range(1, NX):
-        xcopy(dx).start()
-    fx[x] = flux[x // 2, pl.ds(pl.multiple_of(16 * h, 16), 48), :]
-
-    def bcopy(k, t, xx):
-        return remote(
-            msgs.at[k, t, xx],
-            rb.at[k, x, ring[k]],
-            b_send.at[k, t, xx],
-            b_recv.at[k, x, ring[k]],
-            ring_band(k, t),
-            xx,
-        )
-
-    def bcopy_in(k, t, xx):
-        return remote(
-            msgs.at[k, t, xx],
-            rb.at[k, xx, t],
-            b_send.at[k, t, xx],
-            b_recv.at[k, xx, t],
-            ring_band(k, t),
-            xx,
-        )
-
-    def each_b(k, fn):
-        @pl.loop(1, NX)
-        def _(dx):
-            fn(k, ring[k], lax.rem(x + dx, NX))
-
-        @pl.loop(1, n)
-        def _(d):
-            for dx in range(NX):
-                fn(k, lax.rem(ring[k] + d, n), lax.rem(x + dx, NX))
-
-    low = iota((mrows, 128), 1) < 64
-    body_rows = lax.rem(iota((mrows, 128), 0), 16) < 9
-    for k in range(2):
-
-        @pl.loop(1, group)
-        def _(d):
-            acopy_in(k, d).wait_recv()
-
-        flat = gath[k].reshape(mcols, 128)
-        msg = jnp.where(low & body_rows, mm(kmats[k, 0], flat), mm(kmats[k, 1], flat))
-        msgs[k] = msg.astype(BF16).reshape(n, NX, 16, 128)
-        each_b(k, lambda k, t, xx: bcopy(k, t, xx).start())
-        rb[k, x, ring[k]] = msgs[k, ring[k], x]
-
     for dx in range(1, NX):
         xcopy_in(dx).wait_recv()
     for f in range(12):
@@ -559,7 +636,7 @@
             mm(pair_rows, shift_all[:, b * 128 : b * 128 + 128]).astype(BF16).reshape(37, 16, 128)
         )
 
-    @pl.loop(0, 8)
+    @pl.loop(0, 8, unroll=2)
     def _(i):
         left = zbuf[pl.ds(4 * i, 7)].reshape(wide, 128)
         right = zbuf[pl.ds(4 * i + 2, 7)].reshape(wide, 128)
@@ -581,15 +658,15 @@
             acc = acc + jnp.sum(vals * (pre * (1.0 + jnp.tanh(inside))), axis=0, keepdims=True)
         res[i] = acc
 
-    out[x] = jnp.concatenate([res[i] for i in range(8)], axis=0)
+    got_out[x] = jnp.concatenate([res[i] for i in range(8)], axis=0)
 
     def fcopy(dx):
         xx = lax.rem(x + dx, NX)
-        return remote(out.at[x], out.at[x], f_send.at[dx], f_recv.at[x], band, xx)
+        return remote(got_out.at[x], got_out.at[x], f_send.at[dx], f_recv.at[x], band, xx)
 
     def fcopy_in(dx):
         xx = lax.rem(x + dx, NX)
-        return remote(out.at[x], out.at[xx], f_send.at[dx], f_recv.at[xx], band, xx)
+        return remote(got_out.at[x], got_out.at[xx], f_send.at[dx], f_recv.at[xx], band, xx)
 
     for dx in range(1, NX):
         fcopy(dx).start()
@@ -613,6 +690,12 @@
     for dx in range(1, NX):
         fcopy(dx).wait_send()
         fcopy_in(dx).wait_recv()
+    for k in range(2):
+        for i in range(16):
+            lanes = slice(256 * i, 256 * i + 256)
+            out[k : k + 1, lanes] = got_out[2 * k + i // 8, i % 8 : i % 8 + 1, :] * mask_ref[
+                k : k + 1, lanes
+            ].astype(F32)
 
 
 def body(
@@ -636,33 +719,47 @@
     n = side
     group = n * CORES
     pairs = pair_col.shape[0]
-    ints = jnp.concatenate(
-        [tile_owner[None], pair_tile.T, pair_col[None], neighbours.T, tile_owner[None]], axis=0
+    operands = (
+        tile_owner[None],
+        pair_tile.T,
+        pair_col[None],
+        neighbours.T,
+        atmos,
+        remap_lon.transpose(1, 2, 0),
+        remap_lat.transpose(1, 2, 0),
+        stem_w,
+        dw_w,
+        b_in[None],
+        ln_gain[None],
+        head_w[None],
+        w_in,
+        w_out,
+        land_mask,
     )
-    atm = atmos.reshape(12, 45, 32).transpose(2, 0, 1)
-    atm = jnp.pad(atm, ((0, 0), (0, 4), (0, 3))).reshape(512, 48)
-    lat = remap_lat.transpose(2, 1, 0)
-    lon = remap_lon.transpose(1, 2, 0)
-    mask = jnp.tile(land_mask.reshape(2, 64, 64), (1, 1, 3)).astype(F32)
-    small = jnp.stack(
-        [jnp.pad(b_in, (0, 64)), jnp.pad(ln_gain, (0, 208)), jnp.pad(head_w, (0, 208))]
-    )
-    small = jnp.pad(small, ((0, 13), (0, 0)))
     vmem = pltpu.VMEM
     dma = pltpu.SemaphoreType.DMA
     frows = 38 * 16
-    result = pl.pallas_call(
+    return pl.pallas_call(
         functools.partial(kernel, n),
-        out_shape=jax.ShapeDtypeStruct((NX, 8, 256), F32),
-        in_specs=[pl.BlockSpec(memory_space=vmem)] * 10,
+        out_shape=jax.ShapeDtypeStruct((2, 4096), F32),
+        in_specs=[pl.BlockSpec(memory_space=pl.ANY)] * 15,
         out_specs=pl.BlockSpec(memory_space=vmem),
-        scratch_shapes=[
+        scratch_shapes=[vmem(a.shape, a.dtype) for a in operands]
+        + [
+            dma((15,)),
+            vmem((16, 1536), F32),
+            vmem((512, 1536), BF16),
+            vmem((16, 256), F32),
+            vmem((16, 256), BF16),
+            vmem((2, 32, 128), F32),
+            vmem((2, 64, 128), F32),
+            vmem((NX, 8, 256), F32),
             vmem((32, 16, pairs), F32),
             vmem((4, 256, pairs), BF16),
             vmem((2 * group, 4, 2 * n, 256), BF16),
             vmem((2, group, 4, 2 * n, 256), BF16),
-            vmem((2, n, 64, 192), BF16),
-            vmem((2, n, 64, 192), BF16),
+            vmem((2, n, 96, 128), BF16),
+            vmem((2, n, 96, 128), BF16),
             vmem((2, 64, 192), BF16),
             vmem((192, 64), BF16),
             vmem((2, 32, 128), BF16),
@@ -709,8 +806,7 @@
             collective_id=0, has_side_effects=True, vmem_limit_bytes=56 * 1024 * 1024
         ),
         cost_estimate=pl.CostEstimate(flops=4000000000, bytes_accessed=4000000, transcendentals=2000000),
-    )(ints, atm, lat, lon, mask, stem_w, dw_w, small, w_in, w_out)
-    return result.reshape(2, 4096) * land_mask.astype(F32)
+    )(*operands)
 
 
 def solution(mesh):

time: 80.3 us -> 69.9 us (0.87)
  local copies, waits for them, and re-layouts: 6.97 us -> 2.59 us
  Pallas kernels: 70.8 us -> 67.1 us
  other arithmetic: 2.01 us -> 0 us
    pallas_call x1, Pallas kernels: 70.8 us -> 67.1 us  [body(): pl.pallas_call(functools.partial(kernel, n), out_shape=jax.ShapeDtypeStru...]
    unnamed x22 -> x3, local copies, waits for them, and re-layouts: 3.75 us -> 2.03 us
    convert_element_type x3 -> x0, local copies, waits for them, and re-layouts: 0.94 us -> none  [body(): mask = jnp.tile(land_mask.reshape(2, 64, 64), (1, 1, 3)).astype(F32)]
    reshape x2 -> x0, local copies, waits for them, and re-layouts: 0.94 us -> none  [the longest x1 0.79 us: body(): return result.reshape(2, 4096) * land_mask.astype(F32)]
where the time goes in v2:
time: 69.9 us; the launch traced here: 69.7 us
  Pallas kernels  67.1 us (96%)
  local copies, waits for them, and re-layouts  2.59 us (4%)
    pallas_call x1, Pallas kernels, body(): pl.pallas_call(functools.partial(kernel, n), out_shape=jax.ShapeDtypeStru...  67.1 us
    unnamed x3, local copies, waits for them, and re-layouts  2.03 us

profile of v2, /device:TPU:1, one launch (start us, length us, event | category | flops | bytes accessed | tf_op | source)
XLA Modules:
  0.0 69.7 jit_solution(16647257513660633493)
XLA Ops:
  0.0 0.0 copy-start
  0.0 0.7 copy-done
  0.7 0.6 broadcast_in_dim.17.b_in_hbm
  1.2 67.1 %shard_map.145 = f32[2,4096]{1,0:T(2,128)} custom-call(s32[1,256]{1,0:T(1,128)} %bitcast.11, s32[1,256]{1,0:T(1,128)} %bitcast.12, s32[1,256]{1,0:T(1,128)} %bitcast.13, s32[4,256]{1,0:T(4,128)} %bitcast.10, bf16[3,4,1440]{2,1,0:T(4,128)(2,1)} %atm_hbm.1, bf16[32,64,256]{2,1,0:T(8,128)(2,1)} %bitcast.8, bf16[64,4,256]{2,1,0:T(4,128)(2,1)} %bitcast.9, ...), custom_call_target="tpu_custom_call" | custom-call | flops 4000000000 | bytes 4000000 | tf_op jit(solution)/shard_map/pallas_call | solution.py:742
  68.3 1.4 %copy.17 = f32[2,4096]{1,0:T(2,128)} copy(f32[2,4096]{1,0:T(2,128)} %shard_map.145) | data formatting | bytes 65536
Async XLA Ops:
  0.0 0.7 copy-start

commit v3 on v2

--- a/solution.py
+++ b/solution.py
@@ -32,6 +32,10 @@
 
 def mm_tn(a, b):
     return lax.dot_general(a, b, (((0,), (0,)), ((), ())), preferred_element_type=F32)
+
+
+def sdiv(a, b):
+    return lax.div(a, jnp.int32(b))
 
 
 def third(v):
@@ -92,6 +96,7 @@
     kmats,
     msgs,
     rb,
+    edge_sel,
     fx,
     dmat,
     smat,
@@ -125,15 +130,14 @@
     w_recv,
     f_send,
     f_recv,
-    loc_sem,
 ):
     n = side
     group = n * CORES
     band = lax.axis_index("band")
     x = lax.axis_index("chan")
-    y = band // group
+    y = sdiv(band, group)
     zc = lax.rem(band, group)
-    z = zc // CORES
+    z = sdiv(zc, CORES)
     c = lax.rem(zc, CORES)
     mine = (zc, y * CORES + c)
     ring = (y, z)
@@ -144,7 +148,7 @@
     def group_band(k, idx):
         if k == 0:
             return y * group + idx
-        return band_at(idx // CORES, z, lax.rem(idx, CORES))
+        return band_at(sdiv(idx, CORES), z, lax.rem(idx, CORES))
 
     def ring_band(k, t):
         return band_at(t, z, c) if k == 0 else band_at(y, t, c)
@@ -158,6 +162,9 @@
             device_id={"band": tb, "chan": tx},
             device_id_type=MESH,
         )
+
+    def settle(ref, sem):
+        pltpu.make_async_copy(ref, ref, sem).wait()
 
     loads = [
         pltpu.make_async_copy(src, dst, in_sems.at[i])
@@ -285,19 +292,8 @@
         return remote(
             send.at[k * group + idx],
             recv.at[k, mine[k]],
-            p1_send.at[k, idx],
-            p1_recv.at[k, mine[k]],
-            group_band(k, idx),
-            x,
-        )
-
-    def p1_in(k, d):
-        idx = lax.rem(mine[k] + d, group)
-        return remote(
-            send.at[k * group + idx],
-            recv.at[k, idx],
-            p1_send.at[k, idx],
-            p1_recv.at[k, idx],
+            p1_send.at[k],
+            p1_recv.at[k],
             group_band(k, idx),
             x,
         )
@@ -313,7 +309,7 @@
     for i in range(7, 15):
         loads[i].wait()
     small_f[...] = jnp.zeros(small_f.shape, F32)
-    small_f[0:1, 0:192] = b_in[...].astype(F32)
+    small_f[0:1, 0:192] = b_in[...].astype(F32).reshape(1, 192)
     small_f[1:2, 0:48] = ln_gain[...].astype(F32)
     small_f[2:3, 0:48] = head_w[...].astype(F32)
     small[...] = small_f[...].astype(BF16)
@@ -329,12 +325,7 @@
     def share(i, dx):
         src, dst = shares[i]
         xx = lax.rem(x + dx, NX)
-        return remote(src, dst.at[x], w_send.at[i, dx], w_recv.at[i, x], band, xx)
-
-    def share_in(i, dx):
-        src, dst = shares[i]
-        xx = lax.rem(x + dx, NX)
-        return remote(src, dst.at[xx], w_send.at[i, dx], w_recv.at[i, xx], band, xx)
+        return remote(src, dst.at[x], w_send.at[i], w_recv.at[i], band, xx)
 
     for dx in range(1, NX):
         for i in (4, 2, 3, 1, 0):
@@ -392,7 +383,13 @@
         576 + fx_row * 16 + fl_row * 3 + strip_a,
         f_row * 48 + jnp.where(h == 0, r_row - 3, r_row + 13),
     )
-    smat[...] = onehot((want == iota((frows, 640), 1)) & (f_row < 12))
+    smat[...] = onehot((want == iota((frows, 640), 1)) & (f_row < 12) & (want < 576))
+    er_row, er_f = iota((frows, 64), 0) // 16, lax.rem(iota((frows, 64), 0), 16)
+    er_a = jnp.where(h == 0, er_row, er_row - 35)
+    er_to = er_f // 3 * 16 + lax.rem(er_f, 3) * 3 + er_a
+    edge_sel[...] = onehot(
+        (er_to == iota((frows, 64), 1)) & (er_f < 12) & (er_a >= 0) & (er_a <= 2)
+    )
     rr = iota((frows, 128), 0) // 16
     ff = lax.rem(iota((frows, 128), 0), 16)
     ll = iota((frows, 128), 1)
@@ -444,30 +441,17 @@
         return remote(
             agg.at[k, t],
             part.at[k, ring[k]],
-            p2_send.at[k, t],
-            p2_recv.at[k, ring[k]],
+            p2_send.at[k],
+            p2_recv.at[k],
             ring_band(k, t),
             x,
         )
 
-    def p2_in(k, d):
-        t = lax.rem(ring[k] + d, n)
-        return remote(
-            agg.at[k, t],
-            part.at[k, t],
-            p2_send.at[k, t],
-            p2_recv.at[k, t],
-            ring_band(k, t),
-            x,
-        )
-
     krows = group * 8 * n
     k_tile = lax.rem(iota((64, krows), 1) // 2, n)
     for k in range(2):
 
-        @pl.loop(1, group)
-        def _(d):
-            p1_in(k, d).wait_recv()
+        settle(recv.at[k, pl.ds(0, group - 1)], p1_recv.at[k])
 
         got = recv[k].reshape(krows, 256)
         lat_t = got[:, 128:256].astype(F32).T[64:128, :]
@@ -489,14 +473,7 @@
         xx = lax.rem(x + dx, NX)
         at = pl.multiple_of(16 * lax.rem(xx, 2), 16)
         return remote(
-            flux.at[xx // 2, pl.ds(at, 48)], fx.at[x], x_send.at[dx], x_recv.at[x], band, xx
-        )
-
-    def xcopy_in(dx):
-        xx = lax.rem(x + dx, NX)
-        at = pl.multiple_of(16 * lax.rem(xx, 2), 16)
-        return remote(
-            flux.at[xx // 2, pl.ds(at, 48)], fx.at[xx], x_send.at[dx], x_recv.at[xx], band, xx
+            flux.at[sdiv(xx, 2), pl.ds(at, 48)], fx.at[x], x_send.at[0], x_recv.at[0], band, xx
         )
 
     def acopy(k, d):
@@ -504,28 +481,15 @@
         return remote(
             strips.at[k],
             gath.at[k, mine[k]],
-            a_send.at[k, idx],
-            a_recv.at[k, mine[k]],
+            a_send.at[k],
+            a_recv.at[k],
             group_band(k, idx),
             x,
         )
 
-    def acopy_in(k, d):
-        idx = lax.rem(mine[k] + d, group)
-        return remote(
-            strips.at[k],
-            gath.at[k, idx],
-            a_send.at[k, idx],
-            a_recv.at[k, idx],
-            group_band(k, idx),
-            x,
-        )
-
-    for k in range(2):
-
-        @pl.loop(1, n)
-        def _(d):
-            p2_in(k, d).wait_recv()
+    for k in range(2):
+
+        settle(part.at[k, pl.ds(0, n - 1)], p2_recv.at[k])
 
         total = part[k, 0].astype(F32)
         for t in range(1, n):
@@ -551,24 +515,14 @@
 
     for dx in range(1, NX):
         xcopy(dx).start()
-    fx[x] = flux[x // 2, pl.ds(pl.multiple_of(16 * h, 16), 48), :]
+    fx[x] = flux[sdiv(x, 2), pl.ds(pl.multiple_of(16 * h, 16), 48), :]
 
     def bcopy(k, t, xx):
         return remote(
             msgs.at[k, t, xx],
-            rb.at[k, x, ring[k]],
-            b_send.at[k, t, xx],
-            b_recv.at[k, x, ring[k]],
-            ring_band(k, t),
-            xx,
-        )
-
-    def bcopy_in(k, t, xx):
-        return remote(
-            msgs.at[k, t, xx],
-            rb.at[k, xx, t],
-            b_send.at[k, t, xx],
-            b_recv.at[k, xx, t],
+            rb.at[k, x * n + ring[k]],
+            b_send.at[k],
+            b_recv.at[k],
             ring_band(k, t),
             xx,
         )
@@ -587,19 +541,16 @@
     body_rows = lax.rem(iota((mrows, 128), 0), 16) < 9
     for k in range(2):
 
-        @pl.loop(1, group)
-        def _(d):
-            acopy_in(k, d).wait_recv()
+        settle(gath.at[k, pl.ds(0, group - 1)], a_recv.at[k])
 
         flat = gath[k].reshape(mcols, 128)
         msg = jnp.where(low & body_rows, mm(kmats[k, 0], flat), mm(kmats[k, 1], flat))
         msgs[k] = msg.astype(BF16).reshape(n, NX, 16, 128)
         each_b(k, lambda k, t, xx: bcopy(k, t, xx).start())
-        rb[k, x, ring[k]] = msgs[k, ring[k], x]
-
-    for dx in range(1, NX):
-        for i in range(5):
-            share_in(i, dx).wait_recv()
+        rb[k, x * n + ring[k]] = msgs[k, ring[k], x]
+
+    for i, (_, dst) in enumerate(shares):
+        settle(dst.at[pl.ds(0, NX - 1)], w_recv.at[i])
     gains = jnp.zeros((16, 192), F32)
     for i in range(NX):
         put = onehot(iota((256, 192), 1) == jnp.where(iota((256, 192), 0) < 48, iota((256, 192), 0) + 48 * i, -1))
@@ -614,22 +565,24 @@
         bcol[blk, :] = mm_tn(sm_all[i, :, 0:192], row0)
         vcol[blk, :] = 0.5 * mm(o_all[i], head.astype(BF16))
 
-    for dx in range(1, NX):
-        xcopy_in(dx).wait_recv()
+    settle(fx.at[pl.ds(0, NX - 1)], x_recv.at[0])
     for f in range(12):
         dmat[f * 48 : f * 48 + 48, 0:64] = fx[f // 3, :, (f % 3) * 64 : (f % 3) * 64 + 64]
-    for k in range(2):
-        each_b(k, lambda k, t, xx: bcopy_in(k, t, xx).wait_recv())
+    yx[...] = mm(smat[...], dmat[...]).astype(BF16)
+    for k in range(2):
+        settle(rb.at[k, pl.ds(0, NX * n - 1)], b_recv.at[k])
     total = jnp.zeros((NX, 16, 128), F32)
     for k in range(2):
+        arrived = rb[k].reshape(NX, n, 16, 128)
         for t in range(n):
-            total = total + rb[k, :, t].astype(F32)
+            total = total + arrived[:, t].astype(F32)
     edge = total.reshape(64, 128)
-    dmat[576:640, 0:64] = edge[:, 0:64].astype(BF16)
     elow = iota((64, 128), 1) < 64
-    both = jnp.concatenate([jnp.where(elow, edge, 0.0), jnp.where(elow, 0.0, edge)], axis=0)
+    edge_low = jnp.where(elow, edge, 0.0)
+    both = jnp.concatenate([edge_low, jnp.where(elow, 0.0, edge)], axis=0)
     picked = mm_nt(rowsel[0], both.astype(BF16)) * rowsel[1].astype(F32)
-    yx[...] = (mm(smat[...], dmat[...]) + mm(picked.astype(BF16), collapse)).astype(BF16)
+    outer_rows = mm(edge_sel[...], edge_low.astype(BF16)) + mm(picked.astype(BF16), collapse)
+    yx[...] = (yx[...].astype(F32) + outer_rows).astype(BF16)
     pair_rows = jnp.concatenate([yx[0:592, :], yx[16:608, :]], axis=1)
     for b in range(7):
         zbuf[:, b] = (
@@ -662,34 +615,21 @@
 
     def fcopy(dx):
         xx = lax.rem(x + dx, NX)
-        return remote(got_out.at[x], got_out.at[x], f_send.at[dx], f_recv.at[x], band, xx)
-
-    def fcopy_in(dx):
-        xx = lax.rem(x + dx, NX)
-        return remote(got_out.at[x], got_out.at[xx], f_send.at[dx], f_recv.at[xx], band, xx)
+        return remote(got_out.at[x], got_out.at[x], f_send.at[0], f_recv.at[0], band, xx)
 
     for dx in range(1, NX):
         fcopy(dx).start()
 
     for k in range(2):
-
-        @pl.loop(1, group)
-        def _(d):
-            p1(k, d).wait_send()
-            acopy(k, d).wait_send()
-
-        @pl.loop(1, n)
-        def _(d):
-            p2(k, d).wait_send()
-
-        each_b(k, lambda k, t, xx: bcopy(k, t, xx).wait_send())
-    for dx in range(1, NX):
-        xcopy(dx).wait_send()
-        for i in range(5):
-            share(i, dx).wait_send()
-    for dx in range(1, NX):
-        fcopy(dx).wait_send()
-        fcopy_in(dx).wait_recv()
+        settle(send.at[pl.ds(0, group - 1)], p1_send.at[k])
+        settle(part.at[k, pl.ds(0, n - 1)], p2_send.at[k])
+        settle(gath.at[k, pl.ds(0, group - 1)], a_send.at[k])
+        settle(rb.at[k, pl.ds(0, NX * n - 1)], b_send.at[k])
+    settle(fx.at[pl.ds(0, NX - 1)], x_send.at[0])
+    for i, (_, dst) in enumerate(shares):
+        settle(dst.at[pl.ds(0, NX - 1)], w_send.at[i])
+    settle(got_out.at[pl.ds(0, NX - 1)], f_send.at[0])
+    settle(got_out.at[pl.ds(0, NX - 1)], f_recv.at[0])
     for k in range(2):
         for i in range(16):
             lanes = slice(256 * i, 256 * i + 256)
@@ -729,7 +669,7 @@
         remap_lat.transpose(1, 2, 0),
         stem_w,
         dw_w,
-        b_in[None],
+        b_in,
         ln_gain[None],
         head_w[None],
         w_in,
@@ -766,7 +706,8 @@
             vmem((2, group, 32, 128), BF16),
             vmem((2, 2, n * NX * 16, group * 32), BF16),
             vmem((2, n, NX, 16, 128), BF16),
-            vmem((2, NX, n, 16, 128), BF16),
+            vmem((2, NX * n, 16, 128), BF16),
+            vmem((frows, 64), BF16),
             vmem((NX, 48, 192), BF16),
             vmem((640, 128), BF16),
             vmem((frows, 640), BF16),
@@ -786,20 +727,19 @@
             vmem((768, 128), F32),
             vmem((192, 128), F32),
             vmem((8, 1, 256), F32),
-            dma((2, group)),
-            dma((2, group)),
-            dma((2, n)),
-            dma((2, n)),
-            dma((2, group)),
-            dma((2, group)),
-            dma((NX,)),
-            dma((NX,)),
-            dma((2, n, NX)),
-            dma((2, NX, n)),
-            dma((5, NX)),
-            dma((5, NX)),
-            dma((NX,)),
-            dma((NX,)),
+            dma((2,)),
+            dma((2,)),
+            dma((2,)),
+            dma((2,)),
+            dma((2,)),
+            dma((2,)),
+            dma((1,)),
+            dma((1,)),
+            dma((2,)),
+            dma((2,)),
+            dma((5,)),
+            dma((5,)),
+            dma((1,)),
             dma((1,)),
         ],
         compiler_params=pltpu.CompilerParams(

time: 69.9 us -> 65.5 us (0.937)
  Pallas kernels: 67.1 us -> 63.9 us
  local copies, waits for them, and re-layouts: 2.59 us -> 1.38 us
    pallas_call x1, Pallas kernels: 67.1 us -> 63.9 us  [body(): pl.pallas_call(functools.partial(kernel, n), out_shape=jax.ShapeDtypeStru...]
    unnamed x3 -> x1, local copies, waits for them, and re-layouts: 2.03 us -> 1.38 us
where the time goes in v3:
time: 65.5 us; the launch traced here: 65.3 us
  Pallas kernels  63.9 us (98%)
  local copies, waits for them, and re-layouts  1.38 us (2%)
    pallas_call x1, Pallas kernels, body(): pl.pallas_call(functools.partial(kernel, n), out_shape=jax.ShapeDtypeStru...  63.9 us
    unnamed x1, local copies, waits for them, and re-layouts  1.38 us

profile of v3, /device:TPU:1, one launch (start us, length us, event | category | flops | bytes accessed | tf_op | source)
XLA Modules:
  0.0 65.3 jit_solution(549617492285153129)
XLA Ops:
  0.0 63.9 %shard_map.145 = f32[2,4096]{1,0:T(2,128)} custom-call(s32[1,256]{1,0:T(1,128)} %bitcast.11, s32[1,256]{1,0:T(1,128)} %bitcast.12, s32[1,256]{1,0:T(1,128)} %bitcast.13, s32[4,256]{1,0:T(4,128)} %bitcast.10, bf16[3,4,1440]{2,1,0:T(4,128)(2,1)} %atm_hbm.1, bf16[32,64,256]{2,1,0:T(8,128)(2,1)} %bitcast.8, bf16[64,4,256]{2,1,0:T(4,128)(2,1)} %bitcast.9, ...), custom_call_target="tpu_custom_call" | custom-call | flops 4000000000 | bytes 4000000 | tf_op jit(solution)/shard_map/pallas_call | solution.py:682
  63.9 1.4 %copy.17 = f32[2,4096]{1,0:T(2,128)} copy(f32[2,4096]{1,0:T(2,128)} %shard_map.145) | data formatting | bytes 65536

commit v4 on v3

--- a/solution.py
+++ b/solution.py
@@ -82,7 +82,7 @@
     small,
     mrows_ref,
     mask,
-    got_out,
+    cells,
     xw,
     pls,
     send,
@@ -94,6 +94,7 @@
     strips,
     gath,
     kmats,
+    kwe,
     msgs,
     rb,
     edge_sel,
@@ -339,13 +340,13 @@
     near = jnp.concatenate(near_rows + [jnp.zeros((12, tiles), F32)], axis=0).astype(BF16)
     near_at = mm_nt(near, onehot(ui == owner)).astype(BF16)
     mrows = n * NX * 16
-    mcols = group * 32
+    mcols = group * 16
     mr = iota((mrows, tiles), 0)
-    mt, mx, mrho = mr // 64, lax.rem(mr // 16, NX), lax.rem(mr, 16)
+    mt, mx = mr // 64, lax.rem(mr // 16, NX)
     ci = iota((mrows, mcols), 1)
     rho = lax.rem(iota((mrows, mcols), 0), 16)
     to_h = lax.rem(iota((mrows, mcols), 0) // 16, 2)
-    src, src_half, src_rho = ci // 32, lax.rem(ci // 16, 2), lax.rem(ci, 16)
+    src, src_rho = ci // 16, lax.rem(ci, 16)
     for k in range(2):
         to_place = 2 * (ring_band(k, mt)) + mx // 2
         cols = mm_nt(onehot(iota((mrows, tiles), 1) == to_place), near_at).astype(jnp.int32)
@@ -356,13 +357,18 @@
         src_tag = jnp.where(src_rho == rho, src_place + 1, -1)
         col_ns = jnp.where(to_h == 0, cols[:, 0:1], cols[:, 1:2])
         col_we = jnp.where(rho < 9, cols[:, 2:3], cols[:, 3:4])
-        half_we = jnp.where(rho < 9, 0, 1)
-        kmats[k, 0] = onehot((col_ns == src_tag) & (src_half == to_h))
-        kmats[k, 1] = onehot((col_we == src_tag) & (src_half == half_we))
+        ns = onehot(col_ns == src_tag).reshape(n, 2, 2, 16, mcols)
+        for hh in range(2):
+            kmats[k, hh] = ns[:, :, hh].reshape(mrows // 2, mcols)
+        kwe[k] = onehot(col_we == src_tag)
 
     for k in range(2):
         for i in range(32):
             mrows_ref[k, i : i + 1, :] = mask_ref[k : k + 1, 128 * i : 128 * i + 128].astype(F32)
+        for i in range(16):
+            cells[2 * k + i // 8, i % 8 : i % 8 + 1, :] = mask_ref[
+                k : k + 1, 256 * i : 256 * i + 256
+            ].astype(F32)
         mpick = onehot(iota((64, 32), 1) == iota((64, 32), 0) // 2)
         mfull = mm(mpick, mrows_ref[k].astype(BF16))
         mswap = pltpu.roll(mfull, 64, 1)
@@ -543,8 +549,17 @@
 
         settle(gath.at[k, pl.ds(0, group - 1)], a_recv.at[k])
 
-        flat = gath[k].reshape(mcols, 128)
-        msg = jnp.where(low & body_rows, mm(kmats[k, 0], flat), mm(kmats[k, 1], flat))
+        near_s = gath[k, :, 0:16, :]
+        near_n = gath[k, :, 16:32, :]
+        top = iota((group, 16, 128), 1) < 9
+        mixed_we = jnp.where(top, near_s.astype(F32), near_n.astype(F32)).astype(BF16)
+        from_we = mm(kwe[k], mixed_we.reshape(mcols, 128))
+        from_ns = [
+            mm(kmats[k, hh], part_ns.reshape(mcols, 128)).reshape(n, 2, 16, 128)
+            for hh, part_ns in enumerate((near_s, near_n))
+        ]
+        from_ns = jnp.stack(from_ns, axis=2).reshape(mrows, 128)
+        msg = jnp.where(low & body_rows, from_ns, from_we)
         msgs[k] = msg.astype(BF16).reshape(n, NX, 16, 128)
         each_b(k, lambda k, t, xx: bcopy(k, t, xx).start())
         rb[k, x * n + ring[k]] = msgs[k, ring[k], x]
@@ -611,11 +626,11 @@
             acc = acc + jnp.sum(vals * (pre * (1.0 + jnp.tanh(inside))), axis=0, keepdims=True)
         res[i] = acc
 
-    got_out[x] = jnp.concatenate([res[i] for i in range(8)], axis=0)
+    out[x] = jnp.concatenate([res[i] for i in range(8)], axis=0) * cells[x]
 
     def fcopy(dx):
         xx = lax.rem(x + dx, NX)
-        return remote(got_out.at[x], got_out.at[x], f_send.at[0], f_recv.at[0], band, xx)
+        return remote(out.at[x], out.at[x], f_send.at[0], f_recv.at[0], band, xx)
 
     for dx in range(1, NX):
         fcopy(dx).start()
@@ -628,14 +643,8 @@
     settle(fx.at[pl.ds(0, NX - 1)], x_send.at[0])
     for i, (_, dst) in enumerate(shares):
         settle(dst.at[pl.ds(0, NX - 1)], w_send.at[i])
-    settle(got_out.at[pl.ds(0, NX - 1)], f_send.at[0])
-    settle(got_out.at[pl.ds(0, NX - 1)], f_recv.at[0])
-    for k in range(2):
-        for i in range(16):
-            lanes = slice(256 * i, 256 * i + 256)
-            out[k : k + 1, lanes] = got_out[2 * k + i // 8, i % 8 : i % 8 + 1, :] * mask_ref[
-                k : k + 1, lanes
-            ].astype(F32)
+    settle(out.at[pl.ds(0, NX - 1)], f_send.at[0])
+    settle(out.at[pl.ds(0, NX - 1)], f_recv.at[0])
 
 
 def body(
@@ -679,9 +688,9 @@
     vmem = pltpu.VMEM
     dma = pltpu.SemaphoreType.DMA
     frows = 38 * 16
-    return pl.pallas_call(
+    result = pl.pallas_call(
         functools.partial(kernel, n),
-        out_shape=jax.ShapeDtypeStruct((2, 4096), F32),
+        out_shape=jax.ShapeDtypeStruct((NX, 8, 256), F32),
         in_specs=[pl.BlockSpec(memory_space=pl.ANY)] * 15,
         out_specs=pl.BlockSpec(memory_space=vmem),
         scratch_shapes=[vmem(a.shape, a.dtype) for a in operands]
@@ -704,7 +713,8 @@
             vmem((192, 64), BF16),
             vmem((2, 32, 128), BF16),
             vmem((2, group, 32, 128), BF16),
-            vmem((2, 2, n * NX * 16, group * 32), BF16),
+            vmem((2, 2, n * NX * 8, group * 16), BF16),
+            vmem((2, n * NX * 16, group * 16), BF16),
             vmem((2, n, NX, 16, 128), BF16),
             vmem((2, NX * n, 16, 128), BF16),
             vmem((frows, 64), BF16),
@@ -747,6 +757,7 @@
         ),
         cost_estimate=pl.CostEstimate(flops=4000000000, bytes_accessed=4000000, transcendentals=2000000),
     )(*operands)
+    return result.reshape(2, 4096)
 
 
 def solution(mesh):

time: 65.5 us -> 65.4 us (level)
    reshape x0 -> x1, local copies, waits for them, and re-layouts: none -> 1.4 us  [body(): return result.reshape(2, 4096)]
    unnamed x1 -> x0, local copies, waits for them, and re-layouts: 1.38 us -> none
where the time goes in v4:
time: 65.4 us; the launch traced here: 65.1 us
  Pallas kernels  63.6 us (97%)
  local copies, waits for them, and re-layouts  1.4 us (2%)
    pallas_call x1, Pallas kernels, body(): pl.pallas_call(functools.partial(kernel, n), out_shape=jax.ShapeDtypeStru...  63.6 us
    reshape x1, local copies, waits for them, and re-layouts, body(): return result.reshape(2, 4096)  1.4 us

profile of v4, /device:TPU:1, one launch (start us, length us, event | category | flops | bytes accessed | tf_op | source)
XLA Modules:
  0.0 65.1 jit_solution(8736156412362240226)
XLA Ops:
  0.0 63.6 %shard_map.145 = f32[4,8,256]{2,1,0:T(8,128)} custom-call(s32[1,256]{1,0:T(1,128)} %bitcast.11, s32[1,256]{1,0:T(1,128)} %bitcast.12, s32[1,256]{1,0:T(1,128)} %bitcast.13, s32[4,256]{1,0:T(4,128)} %bitcast.10, bf16[3,4,1440]{2,1,0:T(4,128)(2,1)} %atm_hbm.1, bf16[32,64,256]{2,1,0:T(8,128)(2,1)} %bitcast.8, bf16[64,4,256]{2,1,0:T(4,128)(2,1)} %bitcast.9, ...), custom_call_target="tpu_custom_call" | custom-call | flops 4000000000 | bytes 4000000 | tf_op jit(solution)/shard_map/pallas_call | solution.py:691
  63.7 1.4 %reshape.3 = f32[2,4096]{1,0:T(2,128)} reshape(f32[4,8,256]{2,1,0:T(8,128)} %shard_map.145) | data formatting | bytes 65536 | tf_op jit(solution)/shard_map/reshape | solution.py:760
